TPU v7x, 256 devices: a whole 4x4x8 slice. The times are simulated.
256 devices in a mesh: gx: 4 (over z_hi, core), gy: 16 (over x, y), gz: 4 (over z_lo).
Axes of the slice: x: 4, y: 4, z: 8 (z_hi: 2, z_lo: 4; z = z_hi * 4 + z_lo), core: 2. Of those that a mesh axis runs over, the one named last changes fastest.
Arguments:
- features: bfloat16 [4, 16, 8, 128, 128], P('gx', 'gy', 'gz'), may hold values from -24 to 24
- frac: bfloat16 [4, 16, 8, 3, 128], P('gx', 'gy', 'gz'), may hold values from -0.5 to 0.5
- subpoint: int32 [4, 16, 8, 3, 128], P('gx', 'gy', 'gz'), may hold values from 0 to 5
- counts: int32 [4, 16, 8], P('gx', 'gy', 'gz'), may hold values from 32 to 128, as said below
- w_query: bfloat16 [128, 128], replicated, may hold values from -1 to 1
- w_key: bfloat16 [128, 128], replicated, may hold values from -1 to 1
- w_value: bfloat16 [128, 128], replicated, may hold values from -0.5 to 0.5
- rbf_coef: float32 [8], replicated, may hold values from -3 to 3
- w_out: bfloat16 [128, 128], replicated, may hold values from -0.5 to 0.5
- w_charge: bfloat16 [128, 128], replicated, may hold values from -0.5 to 0.5
- mode_weight: bfloat16 [2, 96, 48, 3072], P(None, 'gx', 'gy', 'gz'), may hold values from -18 to 18
- mesh_gain: float32 [128], replicated, may hold values from 0.1 to 1.9
- w_up: bfloat16 [128, 256], replicated, may hold values from -0.5 to 0.5
- w_down: bfloat16 [256, 128], replicated, may hold values from -0.375 to 0.375
Outputs:
- atoms_out: bfloat16 [4, 16, 8, 128, 128], P('gx', 'gy', 'gz')
Inputs may be any that keep to these rules, and one draw needn't show every extreme that they name: `counts`: a cell's atoms fill its first slots; at least 32 atoms in every cell, and some cell holds 128.
All inputs are finite; a program needn't handle non-finite values.
Results may differ from a plain program's by a relative error of at most 0.012.
Values may be sent and summed in bfloat16 or wider, within the bound.
A program may use at most 64 MiB of HBM per device.

v0:
```python
import functools
import math

import jax
import jax.numpy as jnp
import numpy as np
from jax import lax
from jax.experimental import pallas as pl
from jax.experimental.pallas import tpu as pltpu
from jax.sharding import PartitionSpec as P

MESH = pl.DeviceIdType.MESH
F32 = jnp.float32
BF16 = jnp.bfloat16

D = 128
R = 6
NRBF = 8
MX, MY, MZ = 24, 96, 48
NL = 256
LOG2E = math.log2(math.e)


def tables():
    gx, ch, px = np.meshgrid(np.arange(4), np.arange(8), np.arange(8), indexing="ij")
    x_pos, x_ch = (6 * gx + px - 1).reshape(-1), ch.reshape(-1)
    lane = np.arange(NL)
    l_ch, l_kx, l_ok = lane // MX, lane % MX, lane < 8 * MX
    ang = 2 * np.pi / MX * ((x_pos[:, None] * l_kx[None, :]) % MX)
    same = (x_ch[:, None] == l_ch[None, :]) & l_ok[None, :]
    cos_x, sin_x = np.where(same, np.cos(ang), 0.0), np.where(same, np.sin(ang), 0.0)
    fwd_x = np.concatenate([cos_x, -sin_x], axis=1)
    inv_x = np.concatenate([cos_x.T, -sin_x.T], axis=0)

    gz, cell, pz = np.meshgrid(np.arange(4), np.arange(2), np.arange(8), indexing="ij")
    z_pos = (12 * gz + 6 * cell + pz - 1).reshape(-1)
    ang = 2 * np.pi / MZ * ((z_pos[None, :] * np.arange(MZ)[:, None]) % MZ)
    c, s = np.cos(ang), np.sin(ang)
    mat = np.stack([np.stack([c, s], 1), np.stack([-s, c], 1)], axis=1)
    eye = np.eye(8)
    fwd_z = np.einsum("kciz,pq->kcpizq", mat, eye).reshape(MZ * 2 * 8, 2 * 64 * 8)
    mat = np.stack([np.stack([c.T, -s.T], -1), np.stack([s.T, c.T], -1)], axis=0)
    inv_z = np.einsum("czki,pq->czpkiq", mat, eye).reshape(2 * 64 * 8, MZ * 2 * 8)

    gy, py = np.meshgrid(np.arange(16), np.arange(8), indexing="ij")
    y_pos = (6 * gy + py - 1)
    ang = 2 * np.pi / MY * ((y_pos[None] * np.arange(MY)[:, None, None]) % MY)
    c, s = np.cos(ang), np.sin(ang)
    fwd_y = np.stack([np.stack([c, s], 2), np.stack([-s, c], 2)], axis=0)
    fwd_y = fwd_y.reshape(2 * MY, 256)
    ct, st = np.moveaxis(c, 0, -1), np.moveaxis(s, 0, -1)
    inv_y = np.stack([np.stack([ct, -st], 2), np.stack([st, ct], 2)], axis=1)
    inv_y = inv_y.reshape(256, 2 * MY)
    return [jnp.asarray(t, dtype=BF16) for t in (fwd_x, fwd_z, fwd_y, inv_y, inv_z, inv_x)]


def dot_nn(a, b):
    return lax.dot_general(a, b, (((1,), (0,)), ((), ())), preferred_element_type=F32)


def dot_nt(a, b):
    return lax.dot_general(a, b, (((1,), (1,)), ((), ())), preferred_element_type=F32)


def dot_tn(a, b):
    return lax.dot_general(a, b, (((0,), (0,)), ((), ())), preferred_element_type=F32)


def swap_halves(first, second):
    low = lax.broadcasted_iota(jnp.int32, first.shape, 1) < 64
    return (
        jnp.where(low, first, pltpu.roll(second, 64, 1)),
        jnp.where(low, pltpu.roll(first, 64, 1), second),
    )


def stencil(point, sub, frac):
    offset = point - 1.0 - sub
    lower_w = 0.5 * (0.5 - frac) * (0.5 - frac)
    centre_w = 0.75 - frac * frac
    upper_w = 0.5 * (0.5 + frac) * (0.5 + frac)
    zero = jnp.zeros_like(offset)
    return jnp.where(
        offset == -1.0,
        lower_w,
        jnp.where(offset == 0.0, centre_w, jnp.where(offset == 1.0, upper_w, zero)),
    )


def split3(value):
    high = value.astype(BF16).astype(F32)
    rest = value - high
    middle = rest.astype(BF16).astype(F32)
    return high, middle, rest - middle


def kernel(
    feat_ref,
    frac_ref,
    sub_ref,
    counts_ref,
    coef_ref,
    wq_ref,
    wk_ref,
    wv_ref,
    wo_ref,
    wch_ref,
    wsend_ref,
    gain_ref,
    wup_ref,
    wdown_ref,
    fx_ref,
    fz_ref,
    fy_ref,
    iy_ref,
    iz_ref,
    ix_ref,
    out_ref,
    halo,
    s1,
    r1,
    s2,
    r2,
    s3,
    r3,
    s4,
    r4,
    wrecv,
    wf,
    aux,
    x1,
    t2,
    v2,
    wyz,
    wx,
    rep,
    cols,
    qs,
    qaug,
    kaug,
    scores,
    dist,
    vext,
    smax,
    send_sem,
    recv_sem,
    hsend,
    hrecv,
    wsem,
    wrsem,
):
    gx, gy, gz = lax.axis_index("gx"), lax.axis_index("gy"), lax.axis_index("gz")
    me_xz = gz * 4 + gx

    def dev_xz(p):
        return {"gx": lax.rem(p, 4), "gz": lax.div(p, 4)}

    def dev_y(p):
        return {"gy": p}

    def remote(src, dst, ssem, rsem, device):
        return pltpu.make_async_remote_copy(
            src_ref=src, dst_ref=dst, send_sem=ssem, recv_sem=rsem, device_id=device, device_id_type=MESH
        )

    barrier = pltpu.get_barrier_semaphore()
    for off in range(1, 16):
        pl.semaphore_signal(barrier, inc=1, device_id=dev_xz(lax.rem(me_xz + off, 16)), device_id_type=MESH)
        pl.semaphore_signal(barrier, inc=1, device_id=dev_y(lax.rem(gy + off, 16)), device_id_type=MESH)

    lane_row = lax.broadcasted_iota(jnp.int32, (1, 128), 1)
    aux[...] = jnp.zeros_like(aux)
    for c in range(2):
        sub = sub_ref[c].astype(F32)
        frac = frac_ref[c].astype(F32)
        aux[c, 0:3, :] = ((sub + 0.5 + frac) / R).astype(BF16).astype(F32)
        aux[c, 3:4, :] = (lane_row < counts_ref[c]).astype(F32)
        aux[c, 4:7, :] = frac
        aux[c, 7:10, :] = sub
        halo[1, 1, 1 + c, 0:128, :] = feat_ref[c]
        halo[1, 1, 1 + c, 128:144, :] = aux[c].astype(BF16)

    pl.semaphore_wait(barrier, 30)

    def halo_pair(stage, src_up, dst_up, src_down, dst_down, axis, index, count):
        up = remote(src_up, dst_up, hsend.at[stage, 0], hrecv.at[stage, 0], {axis: lax.rem(index + 1, count)})
        down = remote(
            src_down, dst_down, hsend.at[stage, 1], hrecv.at[stage, 1], {axis: lax.rem(index + count - 1, count)}
        )
        up.start()
        down.start()
        return [up, down]

    own = halo.at[1, 1, pl.ds(1, 2)]
    halo_x = halo_pair(
        0, own, halo.at[1, 0, pl.ds(1, 2)], own, halo.at[1, 2, pl.ds(1, 2)], "gx", gx, 4
    )

    row_i = lax.broadcasted_iota(jnp.int32, (128, 1024), 0)
    lane_i = lax.broadcasted_iota(jnp.int32, (128, 1024), 1)
    rep[...] = (lax.shift_right_logical(lane_i, 3) == row_i).astype(F32).astype(BF16)
    eye = (
        lax.broadcasted_iota(jnp.int32, (128, 128), 0) == lax.broadcasted_iota(jnp.int32, (128, 128), 1)
    ).astype(F32).astype(BF16)
    wch = dot_nn(wch_ref[...], rep[...]).astype(BF16)
    point_rows = lax.broadcasted_iota(jnp.int32, (8, 128), 0).astype(F32)
    point_lanes = lax.bitwise_and(lax.broadcasted_iota(jnp.int32, (128, 128), 1), 7).astype(F32)
    spread = []
    for c in range(2):
        cols[c] = dot_nt(eye, aux[c].astype(BF16))
        col = cols[c]
        wy = stencil(point_rows, aux[c, 8:9, :], aux[c, 5:6, :])
        wz = stencil(point_rows, aux[c, 9:10, :], aux[c, 6:7, :])
        wyz[c] = jnp.concatenate([wz[p : p + 1, :] * wy for p in range(8)], axis=0).astype(BF16)
        wx[c] = stencil(point_lanes, col[:, 7:8], col[:, 4:5])
        wxv = wx[c] * col[:, 3:4]
        charge = dot_nn(feat_ref[c], wch)
        scaled = jnp.concatenate(
            [charge[:, 128 * t : 128 * t + 128] * wxv for t in range(8)], axis=1
        ).astype(BF16)
        spread.append(dot_nn(wyz[c], scaled))
    for t in range(8):
        even, odd = swap_halves(
            spread[0][:, 128 * t : 128 * t + 128], spread[1][:, 128 * t : 128 * t + 128]
        )
        s1[2 * t] = even.astype(BF16)
        s1[2 * t + 1] = odd.astype(BF16)

    def exchange(phase, src, dst, me, device):
        copies = []
        for off in range(1, 16):
            p = lax.rem(me + off, 16)
            copy = remote(src.at[p], dst.at[me], send_sem.at[phase, off], recv_sem.at[phase, off], device(p))
            copy.start()
            copies.append(copy)
        dst[me] = src[me]
        return copies

    phase1 = exchange(0, s1, r1, me_xz, dev_xz)

    weights = []
    for off in range(1, 4):
        p = lax.rem(gx + off, 4)
        copy = remote(wsend_ref.at[p], wrecv.at[gx], wsem.at[off], wrsem.at[off], {"gx": p})
        copy.start()
        weights.append(copy)
    wrecv[gx] = wsend_ref[gx]

    for c in range(2):
        qs[c] = dot_nn(feat_ref[c], wq_ref[...]).astype(BF16)
        pos = aux[c, 0:3, :]
        qx, qy, qz = pos[0:1, :], pos[1:2, :], pos[2:3, :] + float(c)
        norm = split3(qx * qx + qy * qy + qz * qz)
        one = jnp.ones((1, 128), F32)
        rows = jnp.concatenate(
            [-2.0 * pos, -2.0 * pos, one, one, one, *norm, -2.0 * c * one, -2.0 * c * one, 0.0 * one, 0.0 * one],
            axis=0,
        )
        qaug[c] = dot_nt(eye, rows.astype(BF16)).astype(BF16)
        smax[c] = jnp.full((128, 128), -jnp.inf, F32)

    for copy in halo_x:
        copy.wait_recv()
    halo_z = halo_pair(
        1, halo.at[1, :, 2], halo.at[1, :, 0], halo.at[1, :, 1], halo.at[1, :, 3], "gz", gz, 4
    )

    for copy in phase1:
        copy.wait_recv()
    for g in range(4):
        for t in range(2):
            first, second = swap_halves(r1[4 * g + 2 * t].astype(F32), r1[4 * g + 2 * t + 1].astype(F32))
            x1[128 * g : 128 * g + 64, 128 * t : 128 * t + 128] = first.astype(BF16)
            x1[128 * g + 64 : 128 * g + 128, 128 * t : 128 * t + 128] = second.astype(BF16)
    field = dot_nn(x1[...], fx_ref[...]).astype(BF16)
    t2[0:512, :] = field[:, 0:NL]
    t2[512:1024, :] = field[:, NL : 2 * NL]
    s2[...] = dot_nn(fz_ref[...], t2[...]).astype(BF16).reshape(16, 48, NL)
    phase2 = exchange(1, s2, r2, gy, dev_y)

    for copy in halo_z:
        copy.wait_recv()
    halo_y = halo_pair(2, halo.at[1], halo.at[0], halo.at[1], halo.at[2], "gy", gy, 16)

    coef = [coef_ref[k] * LOG2E for k in range(NRBF)]
    scale = LOG2E / math.sqrt(D)

    def score_slab(y, x):
        slab = 3 * y + x
        feats = halo[y, x, :, 0:128, :].reshape(512, 128)
        keys = dot_nn(feats, wk_ref[...]).astype(BF16)
        vext[slab, :, 0:128] = dot_nn(feats, wv_ref[...]).astype(BF16)
        vext[slab, :, 128:256] = jnp.ones((512, 128), BF16)
        off_x = (x - 1).astype(F32) if not isinstance(x, int) else float(x - 1)
        off_y = float(y - 1)
        one = jnp.ones((1, 128), F32)
        masks = []
        for z in range(4):
            rows = halo[y, x, z, 128:144, :].astype(F32)
            pos = rows[0:3, :]
            kx, ky, kz = pos[0:1, :] + off_x, pos[1:2, :] + off_y, pos[2:3, :] + float(z - 1)
            norm = split3(kx * kx + ky * ky + kz * kz)
            kaug[:, 128 * z : 128 * z + 128] = jnp.concatenate(
                [
                    pos, off_x * one, off_y * one, float(z - 1) * one, *norm, one, one, one,
                    pos[2:3, :], float(z - 1) * one, 0.0 * one, 0.0 * one,
                ],
                axis=0,
            ).astype(BF16)
            masks.append(jnp.where(rows[3:4, :] > 0.5, 0.0, -jnp.inf))
        mask = jnp.concatenate(masks, axis=1)
        for c in range(2):
            scores[slab, c] = dot_nt(qs[c], keys[128 * c : 128 * c + 384, :])
            dist[c] = dot_nn(qaug[c], kaug[:, 128 * c : 128 * c + 384])
            for r in range(0, 128, 16):
                t = jnp.exp2(dist[c, r : r + 16, :] * (-0.08 * LOG2E))
                powers = [t]
                for k in range(NRBF - 2):
                    powers.append(powers[-1] * powers[-1])
                bias = coef[NRBF - 1] * powers[-1] + coef[NRBF - 2]
                for k in range(NRBF - 3, -1, -1):
                    bias = bias * powers[k] + coef[k]
                bias = bias * t
                full = scores[slab, c, r : r + 16, :] * scale + bias + mask[:, 128 * c : 128 * c + 384]
                scores[slab, c, r : r + 16, :] = full
                top = jnp.maximum(jnp.maximum(full[:, 0:128], full[:, 128:256]), full[:, 256:384])
                smax[c, r : r + 16, :] = jnp.maximum(smax[c, r : r + 16, :], top)

    def score_row(y):
        lax.fori_loop(0, 3, lambda x, carry: (score_slab(y, x), carry)[1], 0)

    score_row(1)

    for copy in weights:
        copy.wait_recv()
    for q in range(4):
        wf[:, :, q] = wrecv[q].astype(F32).reshape(2, 3, 24, NL) * (1.0 / (MX * MY * MZ))
    for copy in phase2:
        copy.wait_recv()
    for j in range(3):
        spectrum = dot_nn(fy_ref[...], r2[:, 16 * j : 16 * j + 16, :].reshape(256, NL))
        real, imag = spectrum[0:MY, :], spectrum[MY : 2 * MY, :]
        w_real, w_imag = wf[0, j].reshape(MY, NL), wf[1, j].reshape(MY, NL)
        mixed = jnp.concatenate(
            [real * w_real - imag * w_imag, real * w_imag + imag * w_real], axis=0
        ).astype(BF16)
        s3[:, 16 * j : 16 * j + 16, :] = dot_nn(iy_ref[...], mixed).astype(BF16).reshape(16, 16, NL)
    phase3 = exchange(2, s3, r3, gy, dev_y)

    for copy in halo_y:
        copy.wait_recv()
    score_row(0)

    for copy in phase3:
        copy.wait_recv()
    back = dot_nn(iz_ref[...], r3[...].reshape(768, NL)).astype(BF16)
    v2[:, 0:NL] = back[0:512, :]
    v2[:, NL : 2 * NL] = back[512:1024, :]
    potential = dot_nn(v2[...], ix_ref[...])
    for g in range(4):
        for t in range(2):
            even, odd = swap_halves(
                potential[128 * g : 128 * g + 64, 128 * t : 128 * t + 128],
                potential[128 * g + 64 : 128 * g + 128, 128 * t : 128 * t + 128],
            )
            s4[4 * g + 2 * t] = even.astype(BF16)
            s4[4 * g + 2 * t + 1] = odd.astype(BF16)
    phase4 = exchange(3, s4, r4, me_xz, dev_xz)

    score_row(2)
    after = []
    for c in range(2):
        top = jnp.max(smax[c], axis=1, keepdims=True)

        def mix(slab, acc, c=c, top=top):
            probs = jnp.exp2(scores[slab, c] - top).astype(BF16)
            return acc + dot_nn(probs, vext[slab, 128 * c : 128 * c + 384, :])

        acc = lax.fori_loop(0, 9, mix, jnp.zeros((128, 256), F32))
        attended = (acc[:, 0:128] / acc[:, 128:256]).astype(BF16)
        after.append(feat_ref[c].astype(F32) + dot_nn(attended, wo_ref[...]))

    for copy in phase4:
        copy.wait_recv()
    fields = [[], []]
    for t in range(8):
        first, second = swap_halves(r4[2 * t].astype(F32), r4[2 * t + 1].astype(F32))
        fields[0].append(first.astype(BF16))
        fields[1].append(second.astype(BF16))
    for c in range(2):
        lines = dot_tn(wyz[c], jnp.concatenate(fields[c], axis=1))
        lines = jnp.concatenate(
            [lines[:, 128 * t : 128 * t + 128] * wx[c] for t in range(8)], axis=1
        ).astype(BF16)
        sampled = dot_nt(lines, rep[...])
        norm_scale = lax.rsqrt(jnp.mean(sampled * sampled, axis=1, keepdims=True) + 1e-06)
        joined = after[c] + sampled * norm_scale * gain_ref[...]
        inner = dot_nn(joined.astype(BF16), wup_ref[...])
        inner = (inner * jax.nn.sigmoid(inner)).astype(BF16)
        result = joined + dot_nn(inner, wdown_ref[...])
        out_ref[c] = jnp.where(cols[c][:, 3:4] > 0.5, result, 0.0).astype(BF16)

    for copy in phase1 + phase2 + phase3 + phase4 + weights + halo_x + halo_z + halo_y:
        copy.wait_send()


def per_device(
    features,
    frac,
    subpoint,
    counts,
    w_query,
    w_key,
    w_value,
    rbf_coef,
    w_out,
    w_charge,
    mode_weight,
    mesh_gain,
    w_up,
    w_down,
):
    wsend = mode_weight.reshape(2, 24, 3, 4, 192)
    wsend = jnp.pad(jnp.transpose(wsend, (3, 0, 2, 1, 4)), ((0, 0),) * 4 + ((0, NL - 192),))
    wsend = wsend.reshape(4, 144, NL)
    vmem = pl.BlockSpec(memory_space=pltpu.VMEM)
    smem = pl.BlockSpec(memory_space=pltpu.SMEM)
    out = pl.pallas_call(
        kernel,
        out_shape=jax.ShapeDtypeStruct((2, 128, 128), BF16),
        in_specs=[vmem, vmem, vmem, smem, smem] + [vmem] * 15,
        out_specs=vmem,
        scratch_shapes=[
            pltpu.VMEM((3, 3, 4, 144, 128), BF16),
            pltpu.VMEM((16, 64, 128), BF16),
            pltpu.VMEM((16, 64, 128), BF16),
            pltpu.VMEM((16, 48, NL), BF16),
            pltpu.VMEM((16, 48, NL), BF16),
            pltpu.VMEM((16, 48, NL), BF16),
            pltpu.VMEM((16, 48, NL), BF16),
            pltpu.VMEM((16, 64, 128), BF16),
            pltpu.VMEM((16, 64, 128), BF16),
            pltpu.VMEM((4, 144, NL), BF16),
            pltpu.VMEM((2, 3, 4, 24, NL), F32),
            pltpu.VMEM((2, 16, 128), F32),
            pltpu.VMEM((512, 256), BF16),
            pltpu.VMEM((1024, NL), BF16),
            pltpu.VMEM((512, 2 * NL), BF16),
            pltpu.VMEM((2, 64, 128), BF16),
            pltpu.VMEM((2, 128, 128), F32),
            pltpu.VMEM((128, 1024), BF16),
            pltpu.VMEM((2, 128, 16), F32),
            pltpu.VMEM((2, 128, 128), BF16),
            pltpu.VMEM((2, 128, 16), BF16),
            pltpu.VMEM((16, 512), BF16),
            pltpu.VMEM((9, 2, 128, 384), F32),
            pltpu.VMEM((2, 128, 384), F32),
            pltpu.VMEM((9, 512, 256), BF16),
            pltpu.VMEM((2, 128, 128), F32),
            pltpu.SemaphoreType.DMA((4, 16)),
            pltpu.SemaphoreType.DMA((4, 16)),
            pltpu.SemaphoreType.DMA((3, 2)),
            pltpu.SemaphoreType.DMA((3, 2)),
            pltpu.SemaphoreType.DMA((4,)),
            pltpu.SemaphoreType.DMA((4,)),
        ],
        compiler_params=pltpu.CompilerParams(
            collective_id=0, has_side_effects=True, vmem_limit_bytes=48 * 1024 * 1024
        ),
    )(
        features.reshape(2, 128, 128),
        frac.reshape(2, 3, 128),
        subpoint.reshape(2, 3, 128),
        counts.reshape(2),
        rbf_coef,
        w_query,
        w_key,
        w_value,
        w_out,
        w_charge,
        wsend,
        mesh_gain.reshape(1, 128),
        w_up,
        w_down,
        *tables(),
    )
    return out.reshape(features.shape)


def solution(mesh):
    return jax.shard_map(
        per_device,
        mesh=mesh,
        in_specs=(
            P("gx", "gy", "gz", None, None),
            P("gx", "gy", "gz", None, None),
            P("gx", "gy", "gz", None, None),
            P("gx", "gy", "gz"),
            P(),
            P(),
            P(),
            P(),
            P(),
            P(),
            P(None, "gx", "gy", "gz"),
            P(),
            P(),
            P(),
        ),
        out_specs=P("gx", "gy", "gz", None, None),
        check_vma=False,
    )
```

profile of v0, /device:TPU:1, one launch (start us, length us, event | category | flops | bytes accessed | tf_op | source)
XLA Modules:
  0.0 75.6 jit_solution(12925249738651825996)
XLA Ops:
  0.0 0.0 copy-start
  0.0 0.0 copy-start.4
  0.0 0.0 copy-start.17
  0.0 0.0 copy-start.18
  0.0 0.0 copy-start.14
  0.0 0.0 copy-start.16
  0.0 0.0 copy-start.15
  0.0 1.3 %reshape.28 = bf16[2,24,3,4,192]{4,3,1,2,0:T(4,128)(2,1)S(1)} reshape(bf16[2,24,3,768]{3,1,2,0:T(8,128)(2,1)} %param.30) | data formatting | bytes 442368 | tf_op jit(solution)/shard_map/reshape | solution.py:423
  1.5 0.0 copy-done.17
  1.5 0.0 copy-done.18
  1.5 0.0 copy-done
  1.5 0.0 copy-done.4
  1.5 0.0 copy-done.14
  1.6 0.0 copy-done.16
  1.6 0.0 copy-done.15
  1.6 0.0 copy-start.1
  1.6 1.4 %copy-done.1 = bf16[1024,768]{1,0:T(8,128)(2,1)S(1)} copy-done((bf16[1024,768]{1,0:T(8,128)(2,1)S(1)}, bf16[1024,768]{1,0:T(8,128)(2,1)}, u32[]{:S(2)}) %copy-start.1) | copy-done | bytes 1572888
  3.0 0.0 copy-start.2
  3.0 0.9 %copy-done.2 = bf16[256,512]{1,0:T(8,128)(2,1)S(1)} copy-done((bf16[256,512]{1,0:T(8,128)(2,1)S(1)}, bf16[256,512]{1,0:T(8,128)(2,1)}, u32[]{:S(2)}) %copy-start.2) | copy-done | bytes 262168
  3.9 0.0 copy-start.3
  3.9 0.9 %copy-done.3 = bf16[512,256]{1,0:T(8,128)(2,1)S(1)} copy-done((bf16[512,256]{1,0:T(8,128)(2,1)S(1)}, bf16[512,256]{1,0:T(8,128)(2,1)}, u32[]{:S(2)}) %copy-start.3) | copy-done | bytes 262168
  4.9 0.0 copy-start.5
  4.9 0.9 %copy-done.5 = bf16[192,256]{1,0:T(8,128)(2,1)S(1)} copy-done((bf16[192,256]{1,0:T(8,128)(2,1)S(1)}, bf16[192,256]{1,0:T(8,128)(2,1)}, u32[]{:S(2)}) %copy-start.5) | copy-done | bytes 98328
  5.8 0.0 copy-start.6
  5.8 0.8 %copy-done.6 = bf16[1,1,2,128,128]{4,3,2,1,0:T(8,128)(2,1)S(1)} copy-done((bf16[1,1,2,128,128]{4,3,2,1,0:T(8,128)(2,1)S(1)}, bf16[1,1,2,128,128]{4,3,2,1,0:T(8,128)(2,1)}, u32[]{:S(2)}) %copy-start.6) | copy-done | bytes 65560
  6.6 0.0 copy-start.7
  6.6 0.8 %copy-done.7 = bf16[128,256]{1,0:T(8,128)(2,1)S(1)} copy-done((bf16[128,256]{1,0:T(8,128)(2,1)S(1)}, bf16[128,256]{1,0:T(8,128)(2,1)}, u32[]{:S(2)}) %copy-start.7) | copy-done | bytes 65560
  7.5 0.0 copy-start.8
  7.5 0.8 %copy-done.8 = bf16[256,128]{1,0:T(8,128)(2,1)S(1)} copy-done((bf16[256,128]{1,0:T(8,128)(2,1)S(1)}, bf16[256,128]{1,0:T(8,128)(2,1)}, u32[]{:S(2)}) %copy-start.8) | copy-done | bytes 65560
  8.3 0.0 copy-start.9
  8.3 0.8 copy-done.9
  9.1 0.0 copy-start.10
  9.1 0.8 copy-done.10
  9.8 0.0 copy-start.11
  9.8 0.8 copy-done.11
  10.6 0.0 copy-start.12
  10.6 0.8 copy-done.12
  11.3 0.0 copy-start.13
  11.3 0.8 copy-done.13
  12.1 62.9 %shard_map.190 = bf16[2,128,128]{2,1,0:T(8,128)(2,1)S(1)} custom-call(bf16[2,128,128]{2,1,0:T(8,128)(2,1)S(1)} %bitcast.20, bf16[2,3,128]{2,1,0:T(4,128)(2,1)S(1)} %bitcast.22, s32[2,3,128]{2,1,0:T(4,128)S(1)} %bitcast.21, s32[2]{0:T(128)S(1)} %bitcast.23, f32[8]{0:T(128)S(1)} %copy-done.15, bf16[128,128]{1,0:T(8,128)(2,1)S(1)} %copy-done.9, ...), custom_call_target="tpu_custom_call" | custom-call | tf_op jit(solution)/shard_map/pallas_call | solution.py:428
  75.0 0.6 copy.31
  (4 shorter events, 0.1 us)
Async XLA Ops:
  0.0 1.5 %copy-start = (bf16[768,1024]{1,0:T(8,128)(2,1)S(1)}, bf16[768,1024]{1,0:T(8,128)(2,1)}, u32[]{:S(2)}) copy-start(bf16[768,1024]{1,0:T(8,128)(2,1)} %constant.16.clone.fz_ref) | copy-start | bytes 4718596
  0.0 1.5 %copy-start.4 = (bf16[256,192]{1,0:T(8,128)(2,1)S(1)}, bf16[256,192]{1,0:T(8,128)(2,1)}, u32[]{:S(2)}) copy-start(bf16[256,192]{1,0:T(8,128)(2,1)} %constant.18.clone.iy_ref) | copy-start | bytes 294916
  0.0 1.5 %copy-start.17 = (s32[1,1,2,3,128]{4,2,3,1,0:T(2,128)S(1)}, s32[1,1,2,3,128]{4,2,3,1,0:T(2,128)}, u32[]{:S(2)}) copy-start(s32[1,1,2,3,128]{4,2,3,1,0:T(2,128)} %param.22) | copy-start | bytes 9220
  0.0 1.5 %copy-start.18 = (bf16[1,1,2,3,128]{4,2,3,1,0:T(2,128)(2,1)S(1)}, bf16[1,1,2,3,128]{4,2,3,1,0:T(2,128)(2,1)}, u32[]{:S(2)}) copy-start(bf16[1,1,2,3,128]{4,2,3,1,0:T(2,128)(2,1)} %param.21) | copy-start | bytes 4612
  0.0 1.5 %copy-start.14 = (s32[1,1,2]{2,1,0:T(1,128)S(1)}, s32[1,1,2]{2,1,0:T(1,128)}, u32[]{:S(2)}) copy-start(s32[1,1,2]{2,1,0:T(1,128)} %param.23) | copy-start | bytes 28
  0.0 1.5 %copy-start.16 = (f32[128]{0:T(128)S(1)}, f32[128]{0:T(128)}, u32[]{:S(2)}) copy-start(f32[128]{0:T(128)} %param.31) | copy-start | bytes 1540
  0.0 1.5 %copy-start.15 = (f32[8]{0:T(128)S(1)}, f32[8]{0:T(128)}, u32[]{:S(2)}) copy-start(f32[8]{0:T(128)} %coef_ref.1) | copy-start | bytes 100
  1.6 1.4 %copy-start.1 = (bf16[1024,768]{1,0:T(8,128)(2,1)S(1)}, bf16[1024,768]{1,0:T(8,128)(2,1)}, u32[]{:S(2)}) copy-start(bf16[1024,768]{1,0:T(8,128)(2,1)} %constant.19.clone.iz_ref) | copy-start | bytes 4718596
  3.0 0.9 %copy-start.2 = (bf16[256,512]{1,0:T(8,128)(2,1)S(1)}, bf16[256,512]{1,0:T(8,128)(2,1)}, u32[]{:S(2)}) copy-start(bf16[256,512]{1,0:T(8,128)(2,1)} %constant.15.clone.fx_ref) | copy-start | bytes 786436
  3.9 0.9 %copy-start.3 = (bf16[512,256]{1,0:T(8,128)(2,1)S(1)}, bf16[512,256]{1,0:T(8,128)(2,1)}, u32[]{:S(2)}) copy-start(bf16[512,256]{1,0:T(8,128)(2,1)} %constant.20.clone.ix_ref) | copy-start | bytes 786436
  4.9 0.9 %copy-start.5 = (bf16[192,256]{1,0:T(8,128)(2,1)S(1)}, bf16[192,256]{1,0:T(8,128)(2,1)}, u32[]{:S(2)}) copy-start(bf16[192,256]{1,0:T(8,128)(2,1)} %constant.17.clone.fy_ref) | copy-start | bytes 294916
  5.8 0.8 %copy-start.6 = (bf16[1,1,2,128,128]{4,3,2,1,0:T(8,128)(2,1)S(1)}, bf16[1,1,2,128,128]{4,3,2,1,0:T(8,128)(2,1)}, u32[]{:S(2)}) copy-start(bf16[1,1,2,128,128]{4,3,2,1,0:T(8,128)(2,1)} %param.20) | copy-start | bytes 196612
  6.6 0.8 %copy-start.7 = (bf16[128,256]{1,0:T(8,128)(2,1)S(1)}, bf16[128,256]{1,0:T(8,128)(2,1)}, u32[]{:S(2)}) copy-start(bf16[128,256]{1,0:T(8,128)(2,1)} %wup_ref.1) | copy-start | bytes 196612
  7.5 0.8 %copy-start.8 = (bf16[256,128]{1,0:T(8,128)(2,1)S(1)}, bf16[256,128]{1,0:T(8,128)(2,1)}, u32[]{:S(2)}) copy-start(bf16[256,128]{1,0:T(8,128)(2,1)} %wdown_ref.1) | copy-start | bytes 196612
  8.3 0.8 %copy-start.9 = (bf16[128,128]{1,0:T(8,128)(2,1)S(1)}, bf16[128,128]{1,0:T(8,128)(2,1)}, u32[]{:S(2)}) copy-start(bf16[128,128]{1,0:T(8,128)(2,1)} %wq_ref.1) | copy-start | bytes 98308
  9.1 0.8 %copy-start.10 = (bf16[128,128]{1,0:T(8,128)(2,1)S(1)}, bf16[128,128]{1,0:T(8,128)(2,1)}, u32[]{:S(2)}) copy-start(bf16[128,128]{1,0:T(8,128)(2,1)} %wk_ref.1) | copy-start | bytes 98308
  9.8 0.8 %copy-start.11 = (bf16[128,128]{1,0:T(8,128)(2,1)S(1)}, bf16[128,128]{1,0:T(8,128)(2,1)}, u32[]{:S(2)}) copy-start(bf16[128,128]{1,0:T(8,128)(2,1)} %wv_ref.1) | copy-start | bytes 98308
  10.6 0.8 %copy-start.12 = (bf16[128,128]{1,0:T(8,128)(2,1)S(1)}, bf16[128,128]{1,0:T(8,128)(2,1)}, u32[]{:S(2)}) copy-start(bf16[128,128]{1,0:T(8,128)(2,1)} %wo_ref.1) | copy-start | bytes 98308
  11.3 0.8 %copy-start.13 = (bf16[128,128]{1,0:T(8,128)(2,1)S(1)}, bf16[128,128]{1,0:T(8,128)(2,1)}, u32[]{:S(2)}) copy-start(bf16[128,128]{1,0:T(8,128)(2,1)} %wch_ref.1) | copy-start | bytes 98308
where the time goes:
time: 76.3 us; the launch traced here: 75.6 us
  Pallas kernels  62.9 us (82%)
  local copies, waits for them, and re-layouts  12.6 us (17%)
    pallas_call x1, Pallas kernels, per_device(): pl.pallas_call(kernel, out_shape=jax.ShapeDtypeStruct((2, 128, 128), BF16...  62.9 us
    unnamed x41, local copies, waits for them, and re-layouts  11.2 us

commit v1 on v0

--- a/solution.py
+++ b/solution.py
@@ -24,13 +24,16 @@
 def tables():
     gx, ch, px = np.meshgrid(np.arange(4), np.arange(8), np.arange(8), indexing="ij")
     x_pos, x_ch = (6 * gx + px - 1).reshape(-1), ch.reshape(-1)
-    lane = np.arange(NL)
-    l_ch, l_kx, l_ok = lane // MX, lane % MX, lane < 8 * MX
-    ang = 2 * np.pi / MX * ((x_pos[:, None] * l_kx[None, :]) % MX)
-    same = (x_ch[:, None] == l_ch[None, :]) & l_ok[None, :]
-    cos_x, sin_x = np.where(same, np.cos(ang), 0.0), np.where(same, np.sin(ang), 0.0)
-    fwd_x = np.concatenate([cos_x, -sin_x], axis=1)
-    inv_x = np.concatenate([cos_x.T, -sin_x.T], axis=0)
+    fwd_x, inv_x = [], []
+    for first in (0, 64):
+        lane = np.arange(NL) - first
+        l_ch, l_kx, l_ok = lane // MX, lane % MX, (lane >= 0) & (lane < 8 * MX)
+        ang = 2 * np.pi / MX * ((x_pos[:, None] * l_kx[None, :]) % MX)
+        same = (x_ch[:, None] == l_ch[None, :]) & l_ok[None, :]
+        cos_x, sin_x = np.where(same, np.cos(ang), 0.0), np.where(same, np.sin(ang), 0.0)
+        fwd_x.append(np.concatenate([cos_x, -sin_x], axis=1))
+        inv_x.append(np.concatenate([cos_x.T, -sin_x.T], axis=0))
+    fwd_x, inv_x = np.stack(fwd_x), np.stack(inv_x)
 
     gz, cell, pz = np.meshgrid(np.arange(4), np.arange(2), np.arange(8), indexing="ij")
     z_pos = (12 * gz + 6 * cell + pz - 1).reshape(-1)
@@ -95,18 +98,33 @@
 
 
 def kernel(
-    feat_ref,
+    feat_hbm,
     frac_ref,
     sub_ref,
     counts_ref,
     coef_ref,
+    gain_ref,
+    wq_hbm,
+    wk_hbm,
+    wv_hbm,
+    wo_hbm,
+    wch_hbm,
+    wup_hbm,
+    wdown_hbm,
+    mode_hbm,
+    fx_hbm,
+    fz_hbm,
+    fy_hbm,
+    iy_hbm,
+    iz_hbm,
+    ix_hbm,
+    out_ref,
+    feat_ref,
     wq_ref,
     wk_ref,
     wv_ref,
     wo_ref,
     wch_ref,
-    wsend_ref,
-    gain_ref,
     wup_ref,
     wdown_ref,
     fx_ref,
@@ -115,7 +133,6 @@
     iy_ref,
     iz_ref,
     ix_ref,
-    out_ref,
     halo,
     s1,
     r1,
@@ -148,6 +165,7 @@
     hrecv,
     wsem,
     wrsem,
+    lsem,
 ):
     gx, gy, gz = lax.axis_index("gx"), lax.axis_index("gy"), lax.axis_index("gz")
     me_xz = gz * 4 + gx
@@ -168,17 +186,46 @@
         pl.semaphore_signal(barrier, inc=1, device_id=dev_xz(lax.rem(me_xz + off, 16)), device_id_type=MESH)
         pl.semaphore_signal(barrier, inc=1, device_id=dev_y(lax.rem(gy + off, 16)), device_id_type=MESH)
 
+    loads = {}
+
+    def load(index, name, src, dst):
+        loads[name] = pltpu.make_async_copy(src, dst, lsem.at[index])
+        loads[name].start()
+
+    def window(p):
+        start = 128 * (lax.div(p, 2) * 3 + lax.rem(p, 2))
+        return mode_hbm.at[:, pl.ds(pl.multiple_of(start, 128), NL)]
+
+    parity = lax.rem(gx, 2)
+    load(0, "feat", feat_hbm, feat_ref)
+    load(1, "wch", wch_hbm, wch_ref)
+    load(2, "wq", wq_hbm, wq_ref)
+    load(3, "fx", fx_hbm.at[parity], fx_ref)
+    load(4, "fz", fz_hbm, fz_ref)
+    load(5, "wk", wk_hbm, wk_ref)
+    load(6, "wv", wv_hbm, wv_ref)
+    load(7, "mode", window(gx), wrecv.at[gx])
+    load(8, "fy", fy_hbm, fy_ref)
+    load(9, "iy", iy_hbm, iy_ref)
+    load(10, "iz", iz_hbm, iz_ref)
+    load(11, "ix", ix_hbm.at[parity], ix_ref)
+    load(12, "wo", wo_hbm, wo_ref)
+    load(13, "wup", wup_hbm, wup_ref)
+    load(14, "wdown", wdown_hbm, wdown_ref)
+
     lane_row = lax.broadcasted_iota(jnp.int32, (1, 128), 1)
     aux[...] = jnp.zeros_like(aux)
     for c in range(2):
-        sub = sub_ref[c].astype(F32)
-        frac = frac_ref[c].astype(F32)
+        sub = jnp.concatenate([sub_ref[d, c : c + 1, :] for d in range(3)], axis=0).astype(F32)
+        frac = jnp.concatenate([frac_ref[d, c : c + 1, :].astype(F32) for d in range(3)], axis=0)
         aux[c, 0:3, :] = ((sub + 0.5 + frac) / R).astype(BF16).astype(F32)
         aux[c, 3:4, :] = (lane_row < counts_ref[c]).astype(F32)
         aux[c, 4:7, :] = frac
         aux[c, 7:10, :] = sub
+        halo[1, 1, 1 + c, 128:144, :] = aux[c].astype(BF16)
+    loads["feat"].wait()
+    for c in range(2):
         halo[1, 1, 1 + c, 0:128, :] = feat_ref[c]
-        halo[1, 1, 1 + c, 128:144, :] = aux[c].astype(BF16)
 
     pl.semaphore_wait(barrier, 30)
 
@@ -202,6 +249,7 @@
     eye = (
         lax.broadcasted_iota(jnp.int32, (128, 128), 0) == lax.broadcasted_iota(jnp.int32, (128, 128), 1)
     ).astype(F32).astype(BF16)
+    loads["wch"].wait()
     wch = dot_nn(wch_ref[...], rep[...]).astype(BF16)
     point_rows = lax.broadcasted_iota(jnp.int32, (8, 128), 0).astype(F32)
     point_lanes = lax.bitwise_and(lax.broadcasted_iota(jnp.int32, (128, 128), 1), 7).astype(F32)
@@ -241,11 +289,11 @@
     weights = []
     for off in range(1, 4):
         p = lax.rem(gx + off, 4)
-        copy = remote(wsend_ref.at[p], wrecv.at[gx], wsem.at[off], wrsem.at[off], {"gx": p})
+        copy = remote(window(p), wrecv.at[gx], wsem.at[off], wrsem.at[off], {"gx": p})
         copy.start()
         weights.append(copy)
-    wrecv[gx] = wsend_ref[gx]
-
+
+    loads["wq"].wait()
     for c in range(2):
         qs[c] = dot_nn(feat_ref[c], wq_ref[...]).astype(BF16)
         pos = aux[c, 0:3, :]
@@ -272,6 +320,8 @@
             first, second = swap_halves(r1[4 * g + 2 * t].astype(F32), r1[4 * g + 2 * t + 1].astype(F32))
             x1[128 * g : 128 * g + 64, 128 * t : 128 * t + 128] = first.astype(BF16)
             x1[128 * g + 64 : 128 * g + 128, 128 * t : 128 * t + 128] = second.astype(BF16)
+    loads["fx"].wait()
+    loads["fz"].wait()
     field = dot_nn(x1[...], fx_ref[...]).astype(BF16)
     t2[0:512, :] = field[:, 0:NL]
     t2[512:1024, :] = field[:, NL : 2 * NL]
@@ -329,10 +379,14 @@
     def score_row(y):
         lax.fori_loop(0, 3, lambda x, carry: (score_slab(y, x), carry)[1], 0)
 
+    loads["wk"].wait()
+    loads["wv"].wait()
     score_row(1)
 
     for copy in weights:
         copy.wait_recv()
+    for name in ("mode", "fy", "iy"):
+        loads[name].wait()
     for q in range(4):
         wf[:, :, q] = wrecv[q].astype(F32).reshape(2, 3, 24, NL) * (1.0 / (MX * MY * MZ))
     for copy in phase2:
@@ -353,6 +407,8 @@
 
     for copy in phase3:
         copy.wait_recv()
+    loads["iz"].wait()
+    loads["ix"].wait()
     back = dot_nn(iz_ref[...], r3[...].reshape(768, NL)).astype(BF16)
     v2[:, 0:NL] = back[0:512, :]
     v2[:, NL : 2 * NL] = back[512:1024, :]
@@ -369,6 +425,8 @@
 
     score_row(2)
     after = []
+    for name in ("wo", "wup", "wdown"):
+        loads[name].wait()
     for c in range(2):
         top = jnp.max(smax[c], axis=1, keepdims=True)
 
@@ -420,17 +478,30 @@
     w_up,
     w_down,
 ):
-    wsend = mode_weight.reshape(2, 24, 3, 4, 192)
-    wsend = jnp.pad(jnp.transpose(wsend, (3, 0, 2, 1, 4)), ((0, 0),) * 4 + ((0, NL - 192),))
-    wsend = wsend.reshape(4, 144, NL)
+    mode_rows = jnp.transpose(mode_weight, (0, 2, 1, 3)).reshape(144, 768)
     vmem = pl.BlockSpec(memory_space=pltpu.VMEM)
     smem = pl.BlockSpec(memory_space=pltpu.SMEM)
+    hbm = pl.BlockSpec(memory_space=pltpu.HBM)
     out = pl.pallas_call(
         kernel,
         out_shape=jax.ShapeDtypeStruct((2, 128, 128), BF16),
-        in_specs=[vmem, vmem, vmem, smem, smem] + [vmem] * 15,
+        in_specs=[hbm, vmem, vmem, smem, smem, vmem] + [hbm] * 14,
         out_specs=vmem,
         scratch_shapes=[
+            pltpu.VMEM((2, 128, 128), BF16),
+            pltpu.VMEM((128, 128), BF16),
+            pltpu.VMEM((128, 128), BF16),
+            pltpu.VMEM((128, 128), BF16),
+            pltpu.VMEM((128, 128), BF16),
+            pltpu.VMEM((128, 128), BF16),
+            pltpu.VMEM((128, 256), BF16),
+            pltpu.VMEM((256, 128), BF16),
+            pltpu.VMEM((256, 2 * NL), BF16),
+            pltpu.VMEM((768, 1024), BF16),
+            pltpu.VMEM((192, 256), BF16),
+            pltpu.VMEM((256, 192), BF16),
+            pltpu.VMEM((1024, 768), BF16),
+            pltpu.VMEM((2 * NL, 256), BF16),
             pltpu.VMEM((3, 3, 4, 144, 128), BF16),
             pltpu.VMEM((16, 64, 128), BF16),
             pltpu.VMEM((16, 64, 128), BF16),
@@ -463,25 +534,26 @@
             pltpu.SemaphoreType.DMA((3, 2)),
             pltpu.SemaphoreType.DMA((4,)),
             pltpu.SemaphoreType.DMA((4,)),
+            pltpu.SemaphoreType.DMA((15,)),
         ],
         compiler_params=pltpu.CompilerParams(
-            collective_id=0, has_side_effects=True, vmem_limit_bytes=48 * 1024 * 1024
+            collective_id=0, has_side_effects=True, vmem_limit_bytes=63 * 1024 * 1024
         ),
     )(
         features.reshape(2, 128, 128),
-        frac.reshape(2, 3, 128),
-        subpoint.reshape(2, 3, 128),
+        jnp.transpose(frac.reshape(2, 3, 128), (1, 0, 2)),
+        jnp.transpose(subpoint.reshape(2, 3, 128), (1, 0, 2)),
         counts.reshape(2),
         rbf_coef,
+        mesh_gain.reshape(1, 128),
         w_query,
         w_key,
         w_value,
         w_out,
         w_charge,
-        wsend,
-        mesh_gain.reshape(1, 128),
         w_up,
         w_down,
+        mode_rows,
         *tables(),
     )
     return out.reshape(features.shape)

time: 76.3 us -> 66 us (0.87)
  local copies, waits for them, and re-layouts: 12.6 us -> 1.47 us
  Pallas kernels: 62.9 us -> 64.4 us
    unnamed x41 -> x1, local copies, waits for them, and re-layouts: 11.2 us -> 1.47 us
    pallas_call x1, Pallas kernels: 62.9 us -> 64.4 us  [per_device(): pl.pallas_call(kernel, out_shape=jax.ShapeDtypeStruct((2, 128, 128), BF16...]
    reshape x2 -> x0, local copies, waits for them, and re-layouts: 1.36 us -> none  [per_device(): wsend = mode_weight.reshape(2, 24, 3, 4, 192)]
where the time goes in v1:
time: 66 us; the launch traced here: 65.9 us
  Pallas kernels  64.4 us (98%)
  local copies, waits for them, and re-layouts  1.47 us (2%)
    pallas_call x1, Pallas kernels, per_device(): pl.pallas_call(kernel, out_shape=jax.ShapeDtypeStruct((2, 128, 128), BF16...  64.4 us
    unnamed x1, local copies, waits for them, and re-layouts  1.47 us

profile of v1, /device:TPU:1, one launch (start us, length us, event | category | flops | bytes accessed | tf_op | source)
XLA Modules:
  0.0 65.9 jit_solution(2797373013591564797)
XLA Ops:
  0.0 64.4 %shard_map.190 = bf16[2,128,128]{2,1,0:T(8,128)(2,1)} custom-call(bf16[2,128,128]{2,1,0:T(8,128)(2,1)} %bitcast.15, bf16[3,2,128]{2,1,0:T(2,128)(2,1)} %bitcast.17, s32[3,2,128]{2,1,0:T(2,128)} %bitcast.16, s32[2]{0:T(128)} %bitcast.18, f32[8]{0:T(128)} %coef_ref.1, f32[1,128]{1,0:T(1,128)} %bitcast.19, bf16[128,128]{1,0:T(8,128)(2,1)} %wq_hbm.1, ...), custom_call_target="tpu_custom_call" | custom-call | tf_op jit(solution)/shard_map/pallas_call | solution.py:485
  64.4 1.5 %copy.22 = bf16[1,1,2,128,128]{4,3,2,1,0:T(8,128)(2,1)} copy(bf16[1,1,2,128,128]{4,3,2,1,0:T(8,128)(2,1)} %bitcast.13) | data formatting | bytes 131072

commit v2 on v1

--- a/solution.py
+++ b/solution.py
@@ -213,6 +213,7 @@
     load(13, "wup", wup_hbm, wup_ref)
     load(14, "wdown", wdown_hbm, wdown_ref)
 
+    mine = lax.div(gx, 2)
     lane_row = lax.broadcasted_iota(jnp.int32, (1, 128), 1)
     aux[...] = jnp.zeros_like(aux)
     for c in range(2):
@@ -222,26 +223,10 @@
         aux[c, 3:4, :] = (lane_row < counts_ref[c]).astype(F32)
         aux[c, 4:7, :] = frac
         aux[c, 7:10, :] = sub
-        halo[1, 1, 1 + c, 128:144, :] = aux[c].astype(BF16)
+        halo[1, mine, 1 + c, 128:144, :] = aux[c].astype(BF16)
     loads["feat"].wait()
     for c in range(2):
-        halo[1, 1, 1 + c, 0:128, :] = feat_ref[c]
-
-    pl.semaphore_wait(barrier, 30)
-
-    def halo_pair(stage, src_up, dst_up, src_down, dst_down, axis, index, count):
-        up = remote(src_up, dst_up, hsend.at[stage, 0], hrecv.at[stage, 0], {axis: lax.rem(index + 1, count)})
-        down = remote(
-            src_down, dst_down, hsend.at[stage, 1], hrecv.at[stage, 1], {axis: lax.rem(index + count - 1, count)}
-        )
-        up.start()
-        down.start()
-        return [up, down]
-
-    own = halo.at[1, 1, pl.ds(1, 2)]
-    halo_x = halo_pair(
-        0, own, halo.at[1, 0, pl.ds(1, 2)], own, halo.at[1, 2, pl.ds(1, 2)], "gx", gx, 4
-    )
+        halo[1, mine, 1 + c, 0:128, :] = feat_ref[c]
 
     row_i = lax.broadcasted_iota(jnp.int32, (128, 1024), 0)
     lane_i = lax.broadcasted_iota(jnp.int32, (128, 1024), 1)
@@ -284,14 +269,20 @@
         dst[me] = src[me]
         return copies
 
+    pl.semaphore_wait(barrier, 30)
     phase1 = exchange(0, s1, r1, me_xz, dev_xz)
 
-    weights = []
-    for off in range(1, 4):
-        p = lax.rem(gx + off, 4)
-        copy = remote(window(p), wrecv.at[gx], wsem.at[off], wrsem.at[off], {"gx": p})
+    halo_copies = []
+
+    def halo_send(index, src, dst, device):
+        copy = remote(src, dst, hsend.at[index], hrecv.at[index], device)
         copy.start()
-        weights.append(copy)
+        halo_copies.append(copy)
+        return copy
+
+    far = 3 - gx
+    own = halo.at[1, mine, pl.ds(1, 2)]
+    halo_far = halo_send(0, own, own, {"gx": far})
 
     loads["wq"].wait()
     for c in range(2):
@@ -307,11 +298,22 @@
         qaug[c] = dot_nt(eye, rows.astype(BF16)).astype(BF16)
         smax[c] = jnp.full((128, 128), -jnp.inf, F32)
 
-    for copy in halo_x:
-        copy.wait_recv()
-    halo_z = halo_pair(
-        1, halo.at[1, :, 2], halo.at[1, :, 0], halo.at[1, :, 1], halo.at[1, :, 3], "gz", gz, 4
-    )
+    halo_far.wait_recv()
+    wrap_up, wrap_down = lax.div(gz + 1, 4), lax.div(4 - gz, 4)
+    dev_up = {"gx": gx + wrap_up * (far - gx), "gz": lax.rem(gz + 1, 4)}
+    dev_down = {"gx": gx + wrap_down * (far - gx), "gz": lax.rem(gz + 3, 4)}
+    pair = pl.ds(0, 2)
+    halo_z = [
+        halo_send(1, halo.at[1, pair, 2], halo.at[1, pair, 0], dev_up),
+        halo_send(2, halo.at[1, pair, 1], halo.at[1, pair, 3], dev_down),
+    ]
+
+    weights = []
+    for off in range(1, 4):
+        p = lax.rem(gx + off, 4)
+        copy = remote(window(p), wrecv.at[gx], wsem.at[off], wrsem.at[off], {"gx": p})
+        copy.start()
+        weights.append(copy)
 
     for copy in phase1:
         copy.wait_recv()
@@ -330,7 +332,15 @@
 
     for copy in halo_z:
         copy.wait_recv()
-    halo_y = halo_pair(2, halo.at[1], halo.at[0], halo.at[1], halo.at[2], "gy", gy, 16)
+    both = halo.at[1, pair]
+    halo_y = [
+        halo_send(3, both, halo.at[0, pair], dev_y(lax.rem(gy + 1, 16))),
+        halo_send(4, both, halo.at[2, pair], dev_y(lax.rem(gy + 15, 16))),
+    ]
+    odd_core = lax.rem(gx, 2)
+    dev_near = {"gx": gx + 1 - 2 * odd_core}
+    halo_near = [halo_send(5, halo.at[1, mine], halo.at[1, 2], dev_near)]
+    near_step = (1 - 2 * odd_core).astype(F32)
 
     coef = [coef_ref[k] * LOG2E for k in range(NRBF)]
     scale = LOG2E / math.sqrt(D)
@@ -341,7 +351,7 @@
         keys = dot_nn(feats, wk_ref[...]).astype(BF16)
         vext[slab, :, 0:128] = dot_nn(feats, wv_ref[...]).astype(BF16)
         vext[slab, :, 128:256] = jnp.ones((512, 128), BF16)
-        off_x = (x - 1).astype(F32) if not isinstance(x, int) else float(x - 1)
+        off_x = near_step if isinstance(x, int) else jnp.where(x == mine, 0.0, -near_step)
         off_y = float(y - 1)
         one = jnp.ones((1, 128), F32)
         masks = []
@@ -376,12 +386,12 @@
                 top = jnp.maximum(jnp.maximum(full[:, 0:128], full[:, 128:256]), full[:, 256:384])
                 smax[c, r : r + 16, :] = jnp.maximum(smax[c, r : r + 16, :], top)
 
-    def score_row(y):
-        lax.fori_loop(0, 3, lambda x, carry: (score_slab(y, x), carry)[1], 0)
+    def score_pair(y):
+        lax.fori_loop(0, 2, lambda x, carry: (score_slab(y, x), carry)[1], 0)
 
     loads["wk"].wait()
     loads["wv"].wait()
-    score_row(1)
+    score_pair(1)
 
     for copy in weights:
         copy.wait_recv()
@@ -403,7 +413,10 @@
 
     for copy in halo_y:
         copy.wait_recv()
-    score_row(0)
+    halo_near.append(halo_send(6, halo.at[0, mine], halo.at[0, 2], dev_near))
+    halo_near.append(halo_send(7, halo.at[2, mine], halo.at[2, 2], dev_near))
+    score_pair(0)
+    score_pair(2)
 
     for copy in phase3:
         copy.wait_recv()
@@ -423,7 +436,9 @@
             s4[4 * g + 2 * t + 1] = odd.astype(BF16)
     phase4 = exchange(3, s4, r4, me_xz, dev_xz)
 
-    score_row(2)
+    for y, copy in zip((1, 0, 2), halo_near):
+        copy.wait_recv()
+        score_slab(y, 2)
     after = []
     for name in ("wo", "wup", "wdown"):
         loads[name].wait()
@@ -458,7 +473,7 @@
         result = joined + dot_nn(inner, wdown_ref[...])
         out_ref[c] = jnp.where(cols[c][:, 3:4] > 0.5, result, 0.0).astype(BF16)
 
-    for copy in phase1 + phase2 + phase3 + phase4 + weights + halo_x + halo_z + halo_y:
+    for copy in phase1 + phase2 + phase3 + phase4 + weights + halo_copies:
         copy.wait_send()
 
 
@@ -530,8 +545,8 @@
             pltpu.VMEM((2, 128, 128), F32),
             pltpu.SemaphoreType.DMA((4, 16)),
             pltpu.SemaphoreType.DMA((4, 16)),
-            pltpu.SemaphoreType.DMA((3, 2)),
-            pltpu.SemaphoreType.DMA((3, 2)),
+            pltpu.SemaphoreType.DMA((8,)),
+            pltpu.SemaphoreType.DMA((8,)),
             pltpu.SemaphoreType.DMA((4,)),
             pltpu.SemaphoreType.DMA((4,)),
             pltpu.SemaphoreType.DMA((15,)),

time: 66 us -> 58.7 us (0.89)
  Pallas kernels: 64.4 us -> 57.1 us
    pallas_call x1, Pallas kernels: 64.4 us -> 57.1 us  [per_device(): pl.pallas_call(kernel, out_shape=jax.ShapeDtypeStruct((2, 128, 128), BF16...]
where the time goes in v2:
time: 58.7 us; the launch traced here: 58.6 us
  Pallas kernels  57.1 us (97%)
  local copies, waits for them, and re-layouts  1.47 us (3%)
    pallas_call x1, Pallas kernels, per_device(): pl.pallas_call(kernel, out_shape=jax.ShapeDtypeStruct((2, 128, 128), BF16...  57.1 us
    unnamed x1, local copies, waits for them, and re-layouts  1.47 us

profile of v2, /device:TPU:1, one launch (start us, length us, event | category | flops | bytes accessed | tf_op | source)
XLA Modules:
  0.0 58.6 jit_solution(17757950391758567110)
XLA Ops:
  0.0 57.1 %shard_map.190 = bf16[2,128,128]{2,1,0:T(8,128)(2,1)} custom-call(bf16[2,128,128]{2,1,0:T(8,128)(2,1)} %bitcast.15, bf16[3,2,128]{2,1,0:T(2,128)(2,1)} %bitcast.17, s32[3,2,128]{2,1,0:T(2,128)} %bitcast.16, s32[2]{0:T(128)} %bitcast.18, f32[8]{0:T(128)} %coef_ref.1, f32[1,128]{1,0:T(1,128)} %bitcast.19, bf16[128,128]{1,0:T(8,128)(2,1)} %wq_hbm.1, ...), custom_call_target="tpu_custom_call" | custom-call | tf_op jit(solution)/shard_map/pallas_call | solution.py:500
  57.1 1.5 %copy.22 = bf16[1,1,2,128,128]{4,3,2,1,0:T(8,128)(2,1)} copy(bf16[1,1,2,128,128]{4,3,2,1,0:T(8,128)(2,1)} %bitcast.13) | data formatting | bytes 131072

commit v3 on v2

--- a/solution.py
+++ b/solution.py
@@ -19,6 +19,9 @@
 MX, MY, MZ = 24, 96, 48
 NL = 256
 LOG2E = math.log2(math.e)
+NEAR = 2
+XZ_STEPS = [(4, 1), (4, 0), (5, 1), (3, 1), (5, 0), (3, 0), (6, 1), (2, 1), (6, 0), (2, 0), (7, 1), (1, 1), (7, 0), (1, 0), (0, 1)]
+Y_STEPS = [(0, 1), (0, 3), (1, 0), (3, 0), (1, 1), (3, 3), (1, 3), (3, 1), (0, 2), (2, 0), (1, 2), (2, 1), (3, 2), (2, 3), (2, 2)]
 
 
 def tables():
@@ -181,10 +184,18 @@
             src_ref=src, dst_ref=dst, send_sem=ssem, recv_sem=rsem, device_id=device, device_id_type=MESH
         )
 
+    z_chip, core = lax.div(gx, 2) * 4 + gz, lax.rem(gx, 2)
+    far_xz, near_y = [], []
+    for step, other in XZ_STEPS:
+        z = lax.rem(z_chip + step, 8)
+        far_xz.append(lax.rem(z, 4) * 4 + lax.div(z, 4) * 2 + (core if other == 0 else 1 - core))
+    for step_x, step_y in Y_STEPS:
+        near_y.append(lax.rem(lax.div(gy, 4) + step_x, 4) * 4 + lax.rem(lax.rem(gy, 4) + step_y, 4))
     barrier = pltpu.get_barrier_semaphore()
-    for off in range(1, 16):
-        pl.semaphore_signal(barrier, inc=1, device_id=dev_xz(lax.rem(me_xz + off, 16)), device_id_type=MESH)
-        pl.semaphore_signal(barrier, inc=1, device_id=dev_y(lax.rem(gy + off, 16)), device_id_type=MESH)
+    for p in far_xz:
+        pl.semaphore_signal(barrier, inc=1, device_id=dev_xz(p), device_id_type=MESH)
+    for p in near_y[::-1]:
+        pl.semaphore_signal(barrier, inc=1, device_id=dev_y(p), device_id_type=MESH)
 
     loads = {}
 
@@ -259,18 +270,17 @@
         s1[2 * t] = even.astype(BF16)
         s1[2 * t + 1] = odd.astype(BF16)
 
-    def exchange(phase, src, dst, me, device):
+    def exchange(phase, src, dst, me, device, partners):
         copies = []
-        for off in range(1, 16):
-            p = lax.rem(me + off, 16)
-            copy = remote(src.at[p], dst.at[me], send_sem.at[phase, off], recv_sem.at[phase, off], device(p))
+        for k, p in enumerate(partners):
+            copy = remote(src.at[p], dst.at[me], send_sem.at[phase, k], recv_sem.at[phase, k], device(p))
             copy.start()
             copies.append(copy)
         dst[me] = src[me]
         return copies
 
     pl.semaphore_wait(barrier, 30)
-    phase1 = exchange(0, s1, r1, me_xz, dev_xz)
+    phase1 = exchange(0, s1, r1, me_xz, dev_xz, far_xz)
 
     halo_copies = []
 
@@ -280,9 +290,25 @@
         halo_copies.append(copy)
         return copy
 
-    far = 3 - gx
-    own = halo.at[1, mine, pl.ds(1, 2)]
-    halo_far = halo_send(0, own, own, {"gx": far})
+    own_slot, far_slot = mine, 1 - mine
+    inner = pl.ds(1, 2)
+    own = halo.at[1, own_slot, inner]
+    up_y, down_y = dev_y(lax.rem(gy + 1, 16)), dev_y(lax.rem(gy + 15, 16))
+    up_z, down_z = {"gz": lax.rem(gz + 1, 4)}, {"gz": lax.rem(gz + 3, 4)}
+
+    def send_z(index, slot):
+        return [
+            halo_send(index, halo.at[1, slot, 2], halo.at[1, slot, 0], up_z),
+            halo_send(index + 1, halo.at[1, slot, 1], halo.at[1, slot, 3], down_z),
+        ]
+
+    def send_y(index, slot, cells):
+        return [
+            halo_send(index, halo.at[1, slot, cells], halo.at[0, slot, cells], up_y),
+            halo_send(index + 1, halo.at[1, slot, cells], halo.at[2, slot, cells], down_y),
+        ]
+
+    own_y = send_y(2, own_slot, inner)
 
     loads["wq"].wait()
     for c in range(2):
@@ -298,23 +324,17 @@
         qaug[c] = dot_nt(eye, rows.astype(BF16)).astype(BF16)
         smax[c] = jnp.full((128, 128), -jnp.inf, F32)
 
-    halo_far.wait_recv()
-    wrap_up, wrap_down = lax.div(gz + 1, 4), lax.div(4 - gz, 4)
-    dev_up = {"gx": gx + wrap_up * (far - gx), "gz": lax.rem(gz + 1, 4)}
-    dev_down = {"gx": gx + wrap_down * (far - gx), "gz": lax.rem(gz + 3, 4)}
-    pair = pl.ds(0, 2)
-    halo_z = [
-        halo_send(1, halo.at[1, pair, 2], halo.at[1, pair, 0], dev_up),
-        halo_send(2, halo.at[1, pair, 1], halo.at[1, pair, 3], dev_down),
-    ]
-
+    for copy in phase1:
+        copy.wait_send()
     weights = []
-    for off in range(1, 4):
+    for off in (2, 1, 3):
         p = lax.rem(gx + off, 4)
         copy = remote(window(p), wrecv.at[gx], wsem.at[off], wrsem.at[off], {"gx": p})
         copy.start()
         weights.append(copy)
 
+    own_z = send_z(0, own_slot)
+    far_copy = halo_send(4, own, own, {"gx": 3 - gx})
     for copy in phase1:
         copy.wait_recv()
     for g in range(4):
@@ -328,18 +348,12 @@
     t2[0:512, :] = field[:, 0:NL]
     t2[512:1024, :] = field[:, NL : 2 * NL]
     s2[...] = dot_nn(fz_ref[...], t2[...]).astype(BF16).reshape(16, 48, NL)
-    phase2 = exchange(1, s2, r2, gy, dev_y)
-
-    for copy in halo_z:
-        copy.wait_recv()
-    both = halo.at[1, pair]
-    halo_y = [
-        halo_send(3, both, halo.at[0, pair], dev_y(lax.rem(gy + 1, 16))),
-        halo_send(4, both, halo.at[2, pair], dev_y(lax.rem(gy + 15, 16))),
-    ]
+    phase2 = exchange(1, s2, r2, gy, dev_y, near_y)
+
+    for copy in own_z:
+        copy.wait_recv()
+    own_y += send_y(5, own_slot, 0) + send_y(7, own_slot, 3)
     odd_core = lax.rem(gx, 2)
-    dev_near = {"gx": gx + 1 - 2 * odd_core}
-    halo_near = [halo_send(5, halo.at[1, mine], halo.at[1, 2], dev_near)]
     near_step = (1 - 2 * odd_core).astype(F32)
 
     coef = [coef_ref[k] * LOG2E for k in range(NRBF)]
@@ -351,7 +365,7 @@
         keys = dot_nn(feats, wk_ref[...]).astype(BF16)
         vext[slab, :, 0:128] = dot_nn(feats, wv_ref[...]).astype(BF16)
         vext[slab, :, 128:256] = jnp.ones((512, 128), BF16)
-        off_x = near_step if isinstance(x, int) else jnp.where(x == mine, 0.0, -near_step)
+        off_x = 0.0 if x is own_slot else (near_step if x is NEAR else -near_step)
         off_y = float(y - 1)
         one = jnp.ones((1, 128), F32)
         masks = []
@@ -386,12 +400,11 @@
                 top = jnp.maximum(jnp.maximum(full[:, 0:128], full[:, 128:256]), full[:, 256:384])
                 smax[c, r : r + 16, :] = jnp.maximum(smax[c, r : r + 16, :], top)
 
-    def score_pair(y):
-        lax.fori_loop(0, 2, lambda x, carry: (score_slab(y, x), carry)[1], 0)
-
     loads["wk"].wait()
     loads["wv"].wait()
-    score_pair(1)
+    score_slab(1, own_slot)
+    far_copy.wait_recv()
+    far_z = send_z(9, far_slot)
 
     for copy in weights:
         copy.wait_recv()
@@ -409,14 +422,19 @@
             [real * w_real - imag * w_imag, real * w_imag + imag * w_real], axis=0
         ).astype(BF16)
         s3[:, 16 * j : 16 * j + 16, :] = dot_nn(iy_ref[...], mixed).astype(BF16).reshape(16, 16, NL)
-    phase3 = exchange(2, s3, r3, gy, dev_y)
-
-    for copy in halo_y:
-        copy.wait_recv()
-    halo_near.append(halo_send(6, halo.at[0, mine], halo.at[0, 2], dev_near))
-    halo_near.append(halo_send(7, halo.at[2, mine], halo.at[2, 2], dev_near))
-    score_pair(0)
-    score_pair(2)
+    phase3 = exchange(2, s3, r3, gy, dev_y, near_y)
+
+    for copy in far_z:
+        copy.wait_recv()
+    far_y = send_y(11, far_slot, pl.ds(0, 4))
+    for copy in own_y:
+        copy.wait_recv()
+    near = halo_send(13, halo.at[:, own_slot], halo.at[:, NEAR], {"gx": gx + 1 - 2 * odd_core})
+    score_slab(0, own_slot)
+    score_slab(2, own_slot)
+    near.wait_recv()
+    for y in range(3):
+        score_slab(y, NEAR)
 
     for copy in phase3:
         copy.wait_recv()
@@ -434,11 +452,13 @@
             )
             s4[4 * g + 2 * t] = even.astype(BF16)
             s4[4 * g + 2 * t + 1] = odd.astype(BF16)
-    phase4 = exchange(3, s4, r4, me_xz, dev_xz)
-
-    for y, copy in zip((1, 0, 2), halo_near):
-        copy.wait_recv()
-        score_slab(y, 2)
+    phase4 = exchange(3, s4, r4, me_xz, dev_xz, far_xz)
+
+    score_slab(1, far_slot)
+    for copy in far_y:
+        copy.wait_recv()
+    score_slab(0, far_slot)
+    score_slab(2, far_slot)
     after = []
     for name in ("wo", "wup", "wdown"):
         loads[name].wait()
@@ -473,7 +493,7 @@
         result = joined + dot_nn(inner, wdown_ref[...])
         out_ref[c] = jnp.where(cols[c][:, 3:4] > 0.5, result, 0.0).astype(BF16)
 
-    for copy in phase1 + phase2 + phase3 + phase4 + weights + halo_copies:
+    for copy in phase2 + phase3 + phase4 + weights + halo_copies:
         copy.wait_send()
 
 
@@ -545,8 +565,8 @@
             pltpu.VMEM((2, 128, 128), F32),
             pltpu.SemaphoreType.DMA((4, 16)),
             pltpu.SemaphoreType.DMA((4, 16)),
-            pltpu.SemaphoreType.DMA((8,)),
-            pltpu.SemaphoreType.DMA((8,)),
+            pltpu.SemaphoreType.DMA((14,)),
+            pltpu.SemaphoreType.DMA((14,)),
             pltpu.SemaphoreType.DMA((4,)),
             pltpu.SemaphoreType.DMA((4,)),
             pltpu.SemaphoreType.DMA((15,)),

time: 58.7 us -> 53.5 us (0.911)
  Pallas kernels: 57.1 us -> 51.9 us
    pallas_call x1, Pallas kernels: 57.1 us -> 51.9 us  [per_device(): pl.pallas_call(kernel, out_shape=jax.ShapeDtypeStruct((2, 128, 128), BF16...]
where the time goes in v3:
time: 53.5 us; the launch traced here: 53.3 us
  Pallas kernels  51.9 us (97%)
  local copies, waits for them, and re-layouts  1.47 us (3%)
    pallas_call x1, Pallas kernels, per_device(): pl.pallas_call(kernel, out_shape=jax.ShapeDtypeStruct((2, 128, 128), BF16...  51.9 us
    unnamed x1, local copies, waits for them, and re-layouts  1.47 us

profile of v3, /device:TPU:1, one launch (start us, length us, event | category | flops | bytes accessed | tf_op | source)
XLA Modules:
  0.0 53.3 jit_solution(17416796180081295725)
XLA Ops:
  0.0 51.9 %shard_map.190 = bf16[2,128,128]{2,1,0:T(8,128)(2,1)} custom-call(bf16[2,128,128]{2,1,0:T(8,128)(2,1)} %bitcast.15, bf16[3,2,128]{2,1,0:T(2,128)(2,1)} %bitcast.17, s32[3,2,128]{2,1,0:T(2,128)} %bitcast.16, s32[2]{0:T(128)} %bitcast.18, f32[8]{0:T(128)} %coef_ref.1, f32[1,128]{1,0:T(1,128)} %bitcast.19, bf16[128,128]{1,0:T(8,128)(2,1)} %wq_hbm.1, ...), custom_call_target="tpu_custom_call" | custom-call | tf_op jit(solution)/shard_map/pallas_call | solution.py:520
  51.9 1.5 %copy.22 = bf16[1,1,2,128,128]{4,3,2,1,0:T(8,128)(2,1)} copy(bf16[1,1,2,128,128]{4,3,2,1,0:T(8,128)(2,1)} %bitcast.13) | data formatting | bytes 131072

commit v4 on v3

--- a/solution.py
+++ b/solution.py
@@ -17,7 +17,7 @@
 R = 6
 NRBF = 8
 MX, MY, MZ = 24, 96, 48
-NL = 256
+NL = 128
 LOG2E = math.log2(math.e)
 NEAR = 2
 XZ_STEPS = [(4, 1), (4, 0), (5, 1), (3, 1), (5, 0), (3, 0), (6, 1), (2, 1), (6, 0), (2, 0), (7, 1), (1, 1), (7, 0), (1, 0), (0, 1)]
@@ -27,16 +27,22 @@
 def tables():
     gx, ch, px = np.meshgrid(np.arange(4), np.arange(8), np.arange(8), indexing="ij")
     x_pos, x_ch = (6 * gx + px - 1).reshape(-1), ch.reshape(-1)
-    fwd_x, inv_x = [], []
-    for first in (0, 64):
-        lane = np.arange(NL) - first
-        l_ch, l_kx, l_ok = lane // MX, lane % MX, (lane >= 0) & (lane < 8 * MX)
-        ang = 2 * np.pi / MX * ((x_pos[:, None] * l_kx[None, :]) % MX)
-        same = (x_ch[:, None] == l_ch[None, :]) & l_ok[None, :]
-        cos_x, sin_x = np.where(same, np.cos(ang), 0.0), np.where(same, np.sin(ang), 0.0)
-        fwd_x.append(np.concatenate([cos_x, -sin_x], axis=1))
-        inv_x.append(np.concatenate([cos_x.T, -sin_x.T], axis=0))
-    fwd_x, inv_x = np.stack(fwd_x), np.stack(inv_x)
+    lane = np.arange(NL)
+    l_ch, l_kx, l_ok = lane // 16, lane % 16, lane % 16 <= MX // 2
+    ang = 2 * np.pi / MX * ((x_pos[:, None] * l_kx[None, :]) % MX)
+    same = (x_ch[:, None] == l_ch[None, :]) & l_ok[None, :]
+    cos_x, sin_x = np.where(same, np.cos(ang), 0.0), np.where(same, np.sin(ang), 0.0)
+    fwd_x = np.concatenate([cos_x, -sin_x], axis=1)
+    inv_x = np.concatenate([cos_x.T, -sin_x.T], axis=0)
+
+    row = np.arange(384)
+    pair_lane = np.arange(2 * NL)
+    l_ch, l_kx = pair_lane // 16, pair_lane % 16
+    share = np.where(l_kx % (MX // 2) == 0, 0.5, 1.0) * (l_kx <= MX // 2)
+    picks = [
+        (row[:, None] == (l_ch * MX + kx)[None, :]) * share[None, :] for kx in (l_kx, (MX - l_kx) % MX)
+    ]
+    pick = np.concatenate(picks, axis=1)
 
     gz, cell, pz = np.meshgrid(np.arange(4), np.arange(2), np.arange(8), indexing="ij")
     z_pos = (12 * gz + 6 * cell + pz - 1).reshape(-1)
@@ -57,7 +63,7 @@
     ct, st = np.moveaxis(c, 0, -1), np.moveaxis(s, 0, -1)
     inv_y = np.stack([np.stack([ct, -st], 2), np.stack([st, ct], 2)], axis=1)
     inv_y = inv_y.reshape(256, 2 * MY)
-    return [jnp.asarray(t, dtype=BF16) for t in (fwd_x, fwd_z, fwd_y, inv_y, inv_z, inv_x)]
+    return [jnp.asarray(t, dtype=BF16) for t in (fwd_x, fwd_z, fwd_y, inv_y, inv_z, inv_x, pick)]
 
 
 def dot_nn(a, b):
@@ -121,6 +127,7 @@
     iy_hbm,
     iz_hbm,
     ix_hbm,
+    pick_hbm,
     out_ref,
     feat_ref,
     wq_ref,
@@ -136,6 +143,11 @@
     iy_ref,
     iz_ref,
     ix_ref,
+    pick_ref,
+    mode_own,
+    mode_first,
+    mode_rest,
+    wsend,
     halo,
     s1,
     r1,
@@ -169,6 +181,8 @@
     wsem,
     wrsem,
     lsem,
+    psend,
+    precv,
 ):
     gx, gy, gz = lax.axis_index("gx"), lax.axis_index("gy"), lax.axis_index("gz")
     me_xz = gz * 4 + gx
@@ -203,23 +217,19 @@
         loads[name] = pltpu.make_async_copy(src, dst, lsem.at[index])
         loads[name].start()
 
-    def window(p):
-        start = 128 * (lax.div(p, 2) * 3 + lax.rem(p, 2))
-        return mode_hbm.at[:, pl.ds(pl.multiple_of(start, 128), NL)]
-
-    parity = lax.rem(gx, 2)
     load(0, "feat", feat_hbm, feat_ref)
     load(1, "wch", wch_hbm, wch_ref)
     load(2, "wq", wq_hbm, wq_ref)
-    load(3, "fx", fx_hbm.at[parity], fx_ref)
+    load(3, "fx", fx_hbm, fx_ref)
     load(4, "fz", fz_hbm, fz_ref)
     load(5, "wk", wk_hbm, wk_ref)
     load(6, "wv", wv_hbm, wv_ref)
-    load(7, "mode", window(gx), wrecv.at[gx])
+    load(7, "mode", mode_hbm, mode_own)
+    load(15, "pick", pick_hbm, pick_ref)
     load(8, "fy", fy_hbm, fy_ref)
     load(9, "iy", iy_hbm, iy_ref)
     load(10, "iz", iz_hbm, iz_ref)
-    load(11, "ix", ix_hbm.at[parity], ix_ref)
+    load(11, "ix", ix_hbm, ix_ref)
     load(12, "wo", wo_hbm, wo_ref)
     load(13, "wup", wup_hbm, wup_ref)
     load(14, "wdown", wdown_hbm, wdown_ref)
@@ -282,6 +292,21 @@
     pl.semaphore_wait(barrier, 30)
     phase1 = exchange(0, s1, r1, me_xz, dev_xz, far_xz)
 
+    mirror, is_own = lax.rem(16 - gy, 16), lax.rem(gy, 8) == 0
+    first_local = pltpu.make_async_copy(mode_hbm.at[:, 0], mode_first, lsem.at[16])
+    first_copy = remote(mode_hbm.at[:, 0], mode_first, psend.at[0], precv.at[0], dev_y(mirror))
+    rest_copy = remote(mode_hbm.at[:, pl.ds(1, 2)], mode_rest, psend.at[1], precv.at[1], dev_y(15 - gy))
+
+    @pl.when(is_own)
+    def _():
+        first_local.start()
+
+    @pl.when(jnp.logical_not(is_own))
+    def _():
+        first_copy.start()
+
+    rest_copy.start()
+
     halo_copies = []
 
     def halo_send(index, src, dst, device):
@@ -326,12 +351,37 @@
 
     for copy in phase1:
         copy.wait_send()
+    loads["mode"].wait()
+    loads["pick"].wait()
+    at_k = mode_own[...].astype(F32).reshape(144, 768).astype(BF16)
+    for t in range(2):
+        picked = dot_nn(at_k[:, 384 * t : 384 * t + 384], pick_ref[:, 0 : 2 * NL]).astype(BF16)
+        for e in range(2):
+            wsend[2 * t + e, :, 0:NL] = picked[:, NL * e : NL * e + NL]
+
+    @pl.when(is_own)
+    def _():
+        first_local.wait()
+
+    @pl.when(jnp.logical_not(is_own))
+    def _():
+        first_copy.wait()
+
+    rest_copy.wait()
+    first = mode_first[...].astype(F32).reshape(2, 1, 24, 768)
+    rest = mode_rest[...].astype(F32)
+    at_minus_k = jnp.concatenate([first, rest[:, 1:2], rest[:, 0:1]], axis=1).reshape(144, 768).astype(BF16)
+    for t in range(2):
+        picked = dot_nn(at_minus_k[:, 384 * t : 384 * t + 384], pick_ref[:, 2 * NL : 4 * NL]).astype(BF16)
+        for e in range(2):
+            wsend[2 * t + e, :, NL : 2 * NL] = picked[:, NL * e : NL * e + NL]
     weights = []
     for off in (2, 1, 3):
         p = lax.rem(gx + off, 4)
-        copy = remote(window(p), wrecv.at[gx], wsem.at[off], wrsem.at[off], {"gx": p})
+        copy = remote(wsend.at[p], wrecv.at[gx], wsem.at[off], wrsem.at[off], {"gx": p})
         copy.start()
         weights.append(copy)
+    wrecv[gx] = wsend[gx]
 
     own_z = send_z(0, own_slot)
     far_copy = halo_send(4, own, own, {"gx": 3 - gx})
@@ -408,20 +458,35 @@
 
     for copy in weights:
         copy.wait_recv()
-    for name in ("mode", "fy", "iy"):
+    for name in ("fy", "iy"):
         loads[name].wait()
     for q in range(4):
-        wf[:, :, q] = wrecv[q].astype(F32).reshape(2, 3, 24, NL) * (1.0 / (MX * MY * MZ))
+        wf[:, :, q] = wrecv[q].astype(F32).reshape(2, 3, 24, 2 * NL) * (1.0 / (MX * MY * MZ))
+    place = lax.broadcasted_iota(jnp.int32, (MY, MY), 0) + lax.broadcasted_iota(jnp.int32, (MY, MY), 1)
+    flip = jnp.logical_or(place == 0, place == MY).astype(F32).astype(BF16)
+    minus = jnp.concatenate(
+        [
+            jnp.concatenate([wrecv[q, 24 * i : 24 * i + 24, NL : 2 * NL].astype(F32) for q in range(4)], axis=0)
+            for i in range(6)
+        ],
+        axis=1,
+    ).astype(BF16)
+    minus = dot_nn(flip, minus) * (1.0 / (MX * MY * MZ))
+    w_real = jnp.concatenate([wf[0, j].reshape(MY, 2 * NL)[:, 0:NL] for j in range(3)], axis=1)
+    w_imag = jnp.concatenate([wf[1, j].reshape(MY, 2 * NL)[:, 0:NL] for j in range(3)], axis=1)
+    w_real = w_real + minus[:, 0 : 3 * NL]
+    w_imag = w_imag - minus[:, 3 * NL : 6 * NL]
     for copy in phase2:
         copy.wait_recv()
+    lines = jnp.concatenate([r2[:, 16 * j : 16 * j + 16, :].reshape(256, NL) for j in range(3)], axis=1)
+    spectrum = dot_nn(fy_ref[...], lines)
+    real, imag = spectrum[0:MY, :], spectrum[MY : 2 * MY, :]
+    mixed = jnp.concatenate(
+        [real * w_real - imag * w_imag, real * w_imag + imag * w_real], axis=0
+    ).astype(BF16)
+    lines = dot_nn(iy_ref[...], mixed).astype(BF16)
     for j in range(3):
-        spectrum = dot_nn(fy_ref[...], r2[:, 16 * j : 16 * j + 16, :].reshape(256, NL))
-        real, imag = spectrum[0:MY, :], spectrum[MY : 2 * MY, :]
-        w_real, w_imag = wf[0, j].reshape(MY, NL), wf[1, j].reshape(MY, NL)
-        mixed = jnp.concatenate(
-            [real * w_real - imag * w_imag, real * w_imag + imag * w_real], axis=0
-        ).astype(BF16)
-        s3[:, 16 * j : 16 * j + 16, :] = dot_nn(iy_ref[...], mixed).astype(BF16).reshape(16, 16, NL)
+        s3[:, 16 * j : 16 * j + 16, :] = lines[:, NL * j : NL * j + NL].reshape(16, 16, NL)
     phase3 = exchange(2, s3, r3, gy, dev_y, near_y)
 
     for copy in far_z:
@@ -513,14 +578,14 @@
     w_up,
     w_down,
 ):
-    mode_rows = jnp.transpose(mode_weight, (0, 2, 1, 3)).reshape(144, 768)
+    mode_rows = jnp.transpose(mode_weight, (0, 2, 1, 3))
     vmem = pl.BlockSpec(memory_space=pltpu.VMEM)
     smem = pl.BlockSpec(memory_space=pltpu.SMEM)
     hbm = pl.BlockSpec(memory_space=pltpu.HBM)
     out = pl.pallas_call(
         kernel,
         out_shape=jax.ShapeDtypeStruct((2, 128, 128), BF16),
-        in_specs=[hbm, vmem, vmem, smem, smem, vmem] + [hbm] * 14,
+        in_specs=[hbm, vmem, vmem, smem, smem, vmem] + [hbm] * 15,
         out_specs=vmem,
         scratch_shapes=[
             pltpu.VMEM((2, 128, 128), BF16),
@@ -537,6 +602,11 @@
             pltpu.VMEM((256, 192), BF16),
             pltpu.VMEM((1024, 768), BF16),
             pltpu.VMEM((2 * NL, 256), BF16),
+            pltpu.VMEM((384, 4 * NL), BF16),
+            pltpu.VMEM((2, 3, 24, 768), BF16),
+            pltpu.VMEM((2, 24, 768), BF16),
+            pltpu.VMEM((2, 2, 24, 768), BF16),
+            pltpu.VMEM((4, 144, 2 * NL), BF16),
             pltpu.VMEM((3, 3, 4, 144, 128), BF16),
             pltpu.VMEM((16, 64, 128), BF16),
             pltpu.VMEM((16, 64, 128), BF16),
@@ -546,8 +616,8 @@
             pltpu.VMEM((16, 48, NL), BF16),
             pltpu.VMEM((16, 64, 128), BF16),
             pltpu.VMEM((16, 64, 128), BF16),
-            pltpu.VMEM((4, 144, NL), BF16),
-            pltpu.VMEM((2, 3, 4, 24, NL), F32),
+            pltpu.VMEM((4, 144, 2 * NL), BF16),
+            pltpu.VMEM((2, 3, 4, 24, 2 * NL), F32),
             pltpu.VMEM((2, 16, 128), F32),
             pltpu.VMEM((512, 256), BF16),
             pltpu.VMEM((1024, NL), BF16),
@@ -569,7 +639,9 @@
             pltpu.SemaphoreType.DMA((14,)),
             pltpu.SemaphoreType.DMA((4,)),
             pltpu.SemaphoreType.DMA((4,)),
-            pltpu.SemaphoreType.DMA((15,)),
+            pltpu.SemaphoreType.DMA((17,)),
+            pltpu.SemaphoreType.DMA((2,)),
+            pltpu.SemaphoreType.DMA((2,)),
         ],
         compiler_params=pltpu.CompilerParams(
             collective_id=0, has_side_effects=True, vmem_limit_bytes=63 * 1024 * 1024

time: 53.5 us -> 55.4 us (1.036)
  Pallas kernels: 51.9 us -> 53.8 us
    pallas_call x1, Pallas kernels: 51.9 us -> 53.8 us  [per_device(): pl.pallas_call(kernel, out_shape=jax.ShapeDtypeStruct((2, 128, 128), BF16...]
where the time goes in v4:
time: 55.4 us; the launch traced here: 55.3 us
  Pallas kernels  53.8 us (97%)
  local copies, waits for them, and re-layouts  1.47 us (3%)
    pallas_call x1, Pallas kernels, per_device(): pl.pallas_call(kernel, out_shape=jax.ShapeDtypeStruct((2, 128, 128), BF16...  53.8 us
    unnamed x1, local copies, waits for them, and re-layouts  1.47 us

profile of v4, /device:TPU:1, one launch (start us, length us, event | category | flops | bytes accessed | tf_op | source)
XLA Modules:
  0.0 55.3 jit_solution(10770173587892430390)
XLA Ops:
  0.0 53.8 %shard_map.199 = bf16[2,128,128]{2,1,0:T(8,128)(2,1)} custom-call(bf16[2,128,128]{2,1,0:T(8,128)(2,1)} %bitcast.13, bf16[3,2,128]{2,1,0:T(2,128)(2,1)} %bitcast.15, s32[3,2,128]{2,1,0:T(2,128)} %bitcast.14, s32[2]{0:T(128)} %bitcast.16, f32[8]{0:T(128)} %coef_ref.1, f32[1,128]{1,0:T(1,128)} %bitcast.17, bf16[128,128]{1,0:T(8,128)(2,1)} %wq_hbm.1, ...), custom_call_target="tpu_custom_call" | custom-call | tf_op jit(solution)/shard_map/pallas_call | solution.py:585
  53.8 1.5 %copy.23 = bf16[1,1,2,128,128]{4,3,2,1,0:T(8,128)(2,1)} copy(bf16[1,1,2,128,128]{4,3,2,1,0:T(8,128)(2,1)} %bitcast.11) | data formatting | bytes 131072

commit v5 on v4

--- a/solution.py
+++ b/solution.py
@@ -158,7 +158,6 @@
     s4,
     r4,
     wrecv,
-    wf,
     aux,
     x1,
     t2,
@@ -351,6 +350,8 @@
 
     for copy in phase1:
         copy.wait_send()
+    own_z = send_z(0, own_slot)
+    far_copy = halo_send(4, own, own, {"gx": 3 - gx})
     loads["mode"].wait()
     loads["pick"].wait()
     at_k = mode_own[...].astype(F32).reshape(144, 768).astype(BF16)
@@ -383,8 +384,6 @@
         weights.append(copy)
     wrecv[gx] = wsend[gx]
 
-    own_z = send_z(0, own_slot)
-    far_copy = halo_send(4, own, own, {"gx": 3 - gx})
     for copy in phase1:
         copy.wait_recv()
     for g in range(4):
@@ -453,29 +452,28 @@
     loads["wk"].wait()
     loads["wv"].wait()
     score_slab(1, own_slot)
-    far_copy.wait_recv()
-    far_z = send_z(9, far_slot)
 
     for copy in weights:
         copy.wait_recv()
     for name in ("fy", "iy"):
         loads[name].wait()
-    for q in range(4):
-        wf[:, :, q] = wrecv[q].astype(F32).reshape(2, 3, 24, 2 * NL) * (1.0 / (MX * MY * MZ))
+    received = [wrecv[q].astype(F32) for q in range(4)]
+
+    def lines_of(first_lane):
+        return [
+            jnp.concatenate(
+                [received[q][24 * i : 24 * i + 24, first_lane : first_lane + NL] for q in range(4)], axis=0
+            )
+            for i in range(6)
+        ]
+
     place = lax.broadcasted_iota(jnp.int32, (MY, MY), 0) + lax.broadcasted_iota(jnp.int32, (MY, MY), 1)
     flip = jnp.logical_or(place == 0, place == MY).astype(F32).astype(BF16)
-    minus = jnp.concatenate(
-        [
-            jnp.concatenate([wrecv[q, 24 * i : 24 * i + 24, NL : 2 * NL].astype(F32) for q in range(4)], axis=0)
-            for i in range(6)
-        ],
-        axis=1,
-    ).astype(BF16)
-    minus = dot_nn(flip, minus) * (1.0 / (MX * MY * MZ))
-    w_real = jnp.concatenate([wf[0, j].reshape(MY, 2 * NL)[:, 0:NL] for j in range(3)], axis=1)
-    w_imag = jnp.concatenate([wf[1, j].reshape(MY, 2 * NL)[:, 0:NL] for j in range(3)], axis=1)
-    w_real = w_real + minus[:, 0 : 3 * NL]
-    w_imag = w_imag - minus[:, 3 * NL : 6 * NL]
+    minus = dot_nn(flip, jnp.concatenate(lines_of(NL), axis=1).astype(BF16))
+    plus = jnp.concatenate(lines_of(0), axis=1)
+    norm = 1.0 / (MX * MY * MZ)
+    w_real = (plus[:, 0 : 3 * NL] + minus[:, 0 : 3 * NL]) * norm
+    w_imag = (plus[:, 3 * NL : 6 * NL] - minus[:, 3 * NL : 6 * NL]) * norm
     for copy in phase2:
         copy.wait_recv()
     lines = jnp.concatenate([r2[:, 16 * j : 16 * j + 16, :].reshape(256, NL) for j in range(3)], axis=1)
@@ -489,17 +487,19 @@
         s3[:, 16 * j : 16 * j + 16, :] = lines[:, NL * j : NL * j + NL].reshape(16, 16, NL)
     phase3 = exchange(2, s3, r3, gy, dev_y, near_y)
 
-    for copy in far_z:
-        copy.wait_recv()
-    far_y = send_y(11, far_slot, pl.ds(0, 4))
     for copy in own_y:
         copy.wait_recv()
     near = halo_send(13, halo.at[:, own_slot], halo.at[:, NEAR], {"gx": gx + 1 - 2 * odd_core})
+    far_copy.wait_recv()
+    far_z = send_z(9, far_slot)
     score_slab(0, own_slot)
     score_slab(2, own_slot)
     near.wait_recv()
     for y in range(3):
         score_slab(y, NEAR)
+    for copy in far_z:
+        copy.wait_recv()
+    far_y = send_y(11, far_slot, pl.ds(0, 4))
 
     for copy in phase3:
         copy.wait_recv()
@@ -617,7 +617,6 @@
             pltpu.VMEM((16, 64, 128), BF16),
             pltpu.VMEM((16, 64, 128), BF16),
             pltpu.VMEM((4, 144, 2 * NL), BF16),
-            pltpu.VMEM((2, 3, 4, 24, 2 * NL), F32),
             pltpu.VMEM((2, 16, 128), F32),
             pltpu.VMEM((512, 256), BF16),
             pltpu.VMEM((1024, NL), BF16),

time: 55.4 us -> 51.7 us (0.933)
  Pallas kernels: 53.8 us -> 50 us
    pallas_call x1, Pallas kernels: 53.8 us -> 50 us  [per_device(): pl.pallas_call(kernel, out_shape=jax.ShapeDtypeStruct((2, 128, 128), BF16...]
where the time goes in v5:
time: 51.7 us; the launch traced here: 51.5 us
  Pallas kernels  50 us (97%)
  local copies, waits for them, and re-layouts  1.47 us (3%)
    pallas_call x1, Pallas kernels, per_device(): pl.pallas_call(kernel, out_shape=jax.ShapeDtypeStruct((2, 128, 128), BF16...  50 us
    unnamed x1, local copies, waits for them, and re-layouts  1.47 us

profile of v5, /device:TPU:1, one launch (start us, length us, event | category | flops | bytes accessed | tf_op | source)
XLA Modules:
  0.0 51.5 jit_solution(11459278147156081567)
XLA Ops:
  0.0 50.0 %shard_map.199 = bf16[2,128,128]{2,1,0:T(8,128)(2,1)} custom-call(bf16[2,128,128]{2,1,0:T(8,128)(2,1)} %bitcast.13, bf16[3,2,128]{2,1,0:T(2,128)(2,1)} %bitcast.15, s32[3,2,128]{2,1,0:T(2,128)} %bitcast.14, s32[2]{0:T(128)} %bitcast.16, f32[8]{0:T(128)} %coef_ref.1, f32[1,128]{1,0:T(1,128)} %bitcast.17, bf16[128,128]{1,0:T(8,128)(2,1)} %wq_hbm.1, ...), custom_call_target="tpu_custom_call" | custom-call | tf_op jit(solution)/shard_map/pallas_call | solution.py:585
  50.0 1.5 %copy.23 = bf16[1,1,2,128,128]{4,3,2,1,0:T(8,128)(2,1)} copy(bf16[1,1,2,128,128]{4,3,2,1,0:T(8,128)(2,1)} %bitcast.11) | data formatting | bytes 131072

commit v6 on v5

--- a/solution.py
+++ b/solution.py
@@ -332,7 +332,6 @@
             halo_send(index + 1, halo.at[1, slot, cells], halo.at[2, slot, cells], down_y),
         ]
 
-    own_y = send_y(2, own_slot, inner)
 
     loads["wq"].wait()
     for c in range(2):
@@ -383,6 +382,7 @@
         copy.start()
         weights.append(copy)
     wrecv[gx] = wsend[gx]
+    own_y = send_y(2, own_slot, inner)
 
     for copy in phase1:
         copy.wait_recv()
@@ -401,6 +401,8 @@
 
     for copy in own_z:
         copy.wait_recv()
+    for copy in phase2:
+        copy.wait_send()
     own_y += send_y(5, own_slot, 0) + send_y(7, own_slot, 3)
     odd_core = lax.rem(gx, 2)
     near_step = (1 - 2 * odd_core).astype(F32)
@@ -453,9 +455,14 @@
     loads["wv"].wait()
     score_slab(1, own_slot)
 
+    loads["fy"].wait()
+    for copy in phase2:
+        copy.wait_recv()
+    lines = jnp.concatenate([r2[:, 16 * j : 16 * j + 16, :].reshape(256, NL) for j in range(3)], axis=1)
+    spectrum = dot_nn(fy_ref[...], lines)
     for copy in weights:
         copy.wait_recv()
-    for name in ("fy", "iy"):
+    for name in ("iy",):
         loads[name].wait()
     received = [wrecv[q].astype(F32) for q in range(4)]
 
@@ -474,10 +481,6 @@
     norm = 1.0 / (MX * MY * MZ)
     w_real = (plus[:, 0 : 3 * NL] + minus[:, 0 : 3 * NL]) * norm
     w_imag = (plus[:, 3 * NL : 6 * NL] - minus[:, 3 * NL : 6 * NL]) * norm
-    for copy in phase2:
-        copy.wait_recv()
-    lines = jnp.concatenate([r2[:, 16 * j : 16 * j + 16, :].reshape(256, NL) for j in range(3)], axis=1)
-    spectrum = dot_nn(fy_ref[...], lines)
     real, imag = spectrum[0:MY, :], spectrum[MY : 2 * MY, :]
     mixed = jnp.concatenate(
         [real * w_real - imag * w_imag, real * w_imag + imag * w_real], axis=0
@@ -558,7 +561,7 @@
         result = joined + dot_nn(inner, wdown_ref[...])
         out_ref[c] = jnp.where(cols[c][:, 3:4] > 0.5, result, 0.0).astype(BF16)
 
-    for copy in phase2 + phase3 + phase4 + weights + halo_copies:
+    for copy in phase3 + phase4 + weights + halo_copies:
         copy.wait_send()
 
 

time: 51.7 us -> 51.4 us (level)
  no operation moved by 1% of the time
where the time goes in v6:
time: 51.4 us; the launch traced here: 51.2 us
  Pallas kernels  49.8 us (97%)
  local copies, waits for them, and re-layouts  1.47 us (3%)
    pallas_call x1, Pallas kernels, per_device(): pl.pallas_call(kernel, out_shape=jax.ShapeDtypeStruct((2, 128, 128), BF16...  49.8 us
    unnamed x1, local copies, waits for them, and re-layouts  1.47 us

profile of v6, /device:TPU:1, one launch (start us, length us, event | category | flops | bytes accessed | tf_op | source)
XLA Modules:
  0.0 51.2 jit_solution(10216287855057263897)
XLA Ops:
  0.0 49.8 %shard_map.199 = bf16[2,128,128]{2,1,0:T(8,128)(2,1)} custom-call(bf16[2,128,128]{2,1,0:T(8,128)(2,1)} %bitcast.13, bf16[3,2,128]{2,1,0:T(2,128)(2,1)} %bitcast.15, s32[3,2,128]{2,1,0:T(2,128)} %bitcast.14, s32[2]{0:T(128)} %bitcast.16, f32[8]{0:T(128)} %coef_ref.1, f32[1,128]{1,0:T(1,128)} %bitcast.17, bf16[128,128]{1,0:T(8,128)(2,1)} %wq_hbm.1, ...), custom_call_target="tpu_custom_call" | custom-call | tf_op jit(solution)/shard_map/pallas_call | solution.py:588
  49.8 1.5 %copy.23 = bf16[1,1,2,128,128]{4,3,2,1,0:T(8,128)(2,1)} copy(bf16[1,1,2,128,128]{4,3,2,1,0:T(8,128)(2,1)} %bitcast.11) | data formatting | bytes 131072

commit v7 on v6

--- a/solution.py
+++ b/solution.py
@@ -165,6 +165,8 @@
     wyz,
     wx,
     rep,
+    rep_t,
+    wyz_t,
     cols,
     qs,
     qaug,
@@ -332,6 +334,12 @@
             halo_send(index + 1, halo.at[1, slot, cells], halo.at[2, slot, cells], down_y),
         ]
 
+
+    row_t = lax.broadcasted_iota(jnp.int32, (1024, 128), 0)
+    lane_t = lax.broadcasted_iota(jnp.int32, (1024, 128), 1)
+    rep_t[...] = (lax.shift_right_logical(row_t, 3) == lane_t).astype(F32).astype(BF16)
+    for c in range(2):
+        wyz_t[c] = dot_nt(eye, wyz[c]).astype(BF16)
 
     loads["wq"].wait()
     for c in range(2):
@@ -549,11 +557,11 @@
         fields[0].append(first.astype(BF16))
         fields[1].append(second.astype(BF16))
     for c in range(2):
-        lines = dot_tn(wyz[c], jnp.concatenate(fields[c], axis=1))
+        lines = dot_nn(wyz_t[c], jnp.concatenate(fields[c], axis=1))
         lines = jnp.concatenate(
             [lines[:, 128 * t : 128 * t + 128] * wx[c] for t in range(8)], axis=1
         ).astype(BF16)
-        sampled = dot_nt(lines, rep[...])
+        sampled = dot_nn(lines, rep_t[...])
         norm_scale = lax.rsqrt(jnp.mean(sampled * sampled, axis=1, keepdims=True) + 1e-06)
         joined = after[c] + sampled * norm_scale * gain_ref[...]
         inner = dot_nn(joined.astype(BF16), wup_ref[...])
@@ -627,6 +635,8 @@
             pltpu.VMEM((2, 64, 128), BF16),
             pltpu.VMEM((2, 128, 128), F32),
             pltpu.VMEM((128, 1024), BF16),
+            pltpu.VMEM((1024, 128), BF16),
+            pltpu.VMEM((2, 128, 64), BF16),
             pltpu.VMEM((2, 128, 16), F32),
             pltpu.VMEM((2, 128, 128), BF16),
             pltpu.VMEM((2, 128, 16), BF16),

time: 51.4 us -> 51.3 us (level)
  no operation moved by 1% of the time
where the time goes in v7:
time: 51.3 us; the launch traced here: 51.1 us
  Pallas kernels  49.7 us (97%)
  local copies, waits for them, and re-layouts  1.47 us (3%)
    pallas_call x1, Pallas kernels, per_device(): pl.pallas_call(kernel, out_shape=jax.ShapeDtypeStruct((2, 128, 128), BF16...  49.7 us
    unnamed x1, local copies, waits for them, and re-layouts  1.47 us

profile of v7, /device:TPU:1, one launch (start us, length us, event | category | flops | bytes accessed | tf_op | source)
XLA Modules:
  0.0 51.1 jit_solution(1072591913877482584)
XLA Ops:
  0.0 49.7 %shard_map.199 = bf16[2,128,128]{2,1,0:T(8,128)(2,1)} custom-call(bf16[2,128,128]{2,1,0:T(8,128)(2,1)} %bitcast.13, bf16[3,2,128]{2,1,0:T(2,128)(2,1)} %bitcast.15, s32[3,2,128]{2,1,0:T(2,128)} %bitcast.14, s32[2]{0:T(128)} %bitcast.16, f32[8]{0:T(128)} %coef_ref.1, f32[1,128]{1,0:T(1,128)} %bitcast.17, bf16[128,128]{1,0:T(8,128)(2,1)} %wq_hbm.1, ...), custom_call_target="tpu_custom_call" | custom-call | tf_op jit(solution)/shard_map/pallas_call | solution.py:596
  49.7 1.5 %copy.23 = bf16[1,1,2,128,128]{4,3,2,1,0:T(8,128)(2,1)} copy(bf16[1,1,2,128,128]{4,3,2,1,0:T(8,128)(2,1)} %bitcast.11) | data formatting | bytes 131072
